TPU v7x, 512 devices: a whole 4x4x16 slice. The times are simulated.
512 devices in a mesh: wide: 64 (over y, z_hi, x), narrow: 8 (over z_lo, core).
Axes of the slice: x: 4, y: 4, z: 16 (z_hi: 4, z_lo: 4; z = z_hi * 4 + z_lo), core: 2. Of those that a mesh axis runs over, the one named last changes fastest.
Arguments:
- velocity: float32 [3, 128, 128, 128], P(None, 'wide', 'narrow'), may hold values from -6 to 6
- cotangents: float32 [4, 3, 128, 128, 128], P(None, None, 'wide', 'narrow'), may hold values from -6 to 6
- lead_table: float32 [8], replicated, may hold values from 0.25 to 4
- lead_index: int32 [4], replicated, may hold values from 0 to 7
- first_kernel: float32 [16, 3, 3, 3, 3], replicated, may hold values from -0.625 to 0.625
- first_bias: float32 [16], replicated, may hold values from -3 to 3
- second_kernel: float32 [3, 16, 3, 3, 3], replicated, may hold values from -0.3125 to 0.3125
Outputs:
- grad_velocity: float32 [3, 128, 128, 128], P(None, 'wide', 'narrow')
- grad_first_kernel: float32 [16, 3, 3, 3, 3], replicated
- grad_first_bias: float32 [16], replicated
- grad_second_kernel: float32 [3, 16, 3, 3, 3], replicated
All inputs are finite; a program needn't handle non-finite values.
Results may differ from a plain program's by a relative error of at most 0.0003.
Values sent between devices are 32-bit elements; how exact they have to be, the bound alone decides.
A program may use at most 64 MiB of HBM per device.

v0:
```python
import math

import jax
import jax.numpy as jnp
import ml_dtypes
import numpy as np
from jax import lax
from jax.experimental import pallas as pl
from jax.experimental.pallas import tpu as pltpu
from jax.sharding import PartitionSpec as P

F32 = jnp.float32
BF16 = jnp.bfloat16
MESH = pl.DeviceIdType.MESH
N = 128
WIDE = 64
NARROW = 8
STEP = 0.25


def basis(kind, wave):
    cell = np.arange(N)
    if kind == 0 and wave == 0:
        return np.full(N, 1.0 / math.sqrt(N))
    if kind == 1 and wave == 0:
        return (1.0 - 2.0 * (cell % 2)) / math.sqrt(N)
    angle = 2.0 * np.pi * (cell * wave % N) / N
    return math.sqrt(2.0 / N) * (np.cos(angle) if kind == 0 else np.sin(angle))


def halves(table):
    high = table.astype(np.float32).astype(ml_dtypes.bfloat16)
    low = (table - high.astype(np.float64)).astype(np.float32).astype(ml_dtypes.bfloat16)
    return np.stack([high, low])


def tables():
    tz = np.stack([basis(i % 2, i // 2) for i in range(N)])
    tx = np.stack([basis((i % 16) // 8, 8 * (i // 16) + i % 8) for i in range(N)])
    ty = np.stack([basis(i // 64, i % 64) for i in range(N)])
    ex = np.concatenate([tx[:, 0::2], tx[:, 1::2]], axis=0)
    rows = []
    for n in range(NARROW):
        cells = [16 * n + r for r in range(16)] + [16 * n - 1, 16 * n + 16]
        for y in cells:
            rows.append(ty[:, y % N])
        rows.extend([np.zeros(N)] * 6)
    tyi = np.stack(rows)
    txi = np.stack([tx[:, (2 * w - 1 + x) % N] for w in range(WIDE) for x in range(4)])
    zi = np.concatenate([tz[0::2], tz[1::2]], axis=1)
    spread = np.zeros((2, 2, N, 256))
    gather = np.zeros((2, 2, 144, N))
    for x in range(2):
        for c in range(3):
            for dx in range(3):
                for dy in range(3):
                    for dz in range(3):
                        flat = c * 27 + dx * 9 + dy * 3 + dz
                        lane = (dy * 3 + dz) * 16 + 4 * (x + dx) + c
                        back = ((2 - dy) * 3 + 2 - dz) * 16 + 4 * (x + 2 - dx) + c
                        spread[0, x, flat, lane] = 1.0
                        spread[1, x, flat, back] = 1.0
                        gather[0, x, lane, flat] = 1.0
                        gather[1, x, back, flat] = 1.0
        spread[0, x, 81, 4 * 16 + 3] = 1.0
        gather[0, x, 4 * 16 + 3, 81] = 1.0
    exact = ml_dtypes.bfloat16
    return (
        halves(tz),
        halves(ex),
        halves(ty),
        halves(tyi),
        halves(txi),
        halves(zi),
        spread.astype(exact),
        gather.astype(exact),
    )


def split(value):
    high = value.astype(BF16)
    return high, (value - high.astype(F32)).astype(BF16)


def dot(a, b, dims):
    return lax.dot_general(
        a, b, (((dims[0],), (dims[1],)), ((), ())), preferred_element_type=F32
    )


def dot3(a, b, dims=(1, 0)):
    return dot(a[0], b[0], dims) + dot(a[0], b[1], dims) + dot(a[1], b[0], dims)


def both(ref):
    return ref[0], ref[1]


def roll(value, shift):
    return pltpu.roll(value, shift % value.shape[1], 1)


def lanes():
    return lax.broadcasted_iota(jnp.int32, (1, N), 1)


def swap_blocks(m):
    m = m.T
    lane = lanes()
    for bit in (1, 2, 4):
        size = 16 * bit
        odd = (lane // size) % 2 == 1
        parts = []
        for i in range(0, N, 2 * size):
            low, high = m[i : i + size], m[i + size : i + 2 * size]
            parts.append(jnp.where(odd, roll(high, size), low))
            parts.append(jnp.where(odd, high, roll(low, -size)))
        m = jnp.concatenate(parts, axis=0)
    return m


def x_transform(received, ex):
    pair = jnp.concatenate(received, axis=1)
    big = dot3(ex, split(pair))
    lane = lanes()
    first = big[:N, :N] + roll(big[N:, :N], -48)
    second = roll(big[:N, N:], 48) + big[N:, N:]
    return jnp.where(lane < 48, first, jnp.where(lane < 96, second, 0.0))


def project(field, w, n):
    lane = lanes()
    row = lax.broadcasted_iota(jnp.int32, (N, 1), 0)
    block = lane // 16
    comp = block % 3
    is_sin_z = block // 3 % 2 == 1
    slot = lane % 16
    inside = lane < 96
    wave_x = 8 * n + slot % 8
    nyq_x = jnp.logical_and(slot == 8, n == 0)
    nyq_y = row == 64
    nyq_z = jnp.logical_and(is_sin_z, w == 0)
    kx = jnp.where(nyq_x, 64, wave_x).astype(F32)
    ky = jnp.where(nyq_y, 64, row % 64).astype(F32)
    kz = jnp.where(nyq_z, 64, w).astype(F32)
    inverse = 1.0 / jnp.maximum(kx * kx + ky * ky + kz * kz, 1.0)
    dx = jnp.where(slot < 8, wave_x, -wave_x).astype(F32)
    dy = jnp.where(row < 64, row % 64, -(row % 64)).astype(F32)
    dz = jnp.where(is_sin_z, -w, w).astype(F32)
    nyquist = jnp.where(
        comp == 0,
        jnp.where(nyq_x, 64.0, 0.0),
        jnp.where(comp == 2, jnp.where(nyq_z, 64.0, 0.0), 0.0),
    )
    nyquist = nyquist + jnp.where(jnp.logical_and(comp == 1, nyq_y), 64.0, 0.0)

    def derive(v):
        along_x = dx * jnp.where(slot < 8, roll(v, -8), roll(v, 8))
        along_y = dy * jnp.concatenate([v[64:], v[:64]], axis=0)
        along_z = dz * jnp.where(is_sin_z, roll(v, 48), roll(v, -48))
        return jnp.where(comp == 0, along_x, jnp.where(comp == 1, along_y, along_z))

    def over_components(v):
        total = (v + roll(v, -16) + roll(v, -32)) * inverse
        total = jnp.where(jnp.logical_and(inside, comp == 0), total, 0.0)
        return total + roll(total, 16) + roll(total, 32)

    main = over_components(derive(field))
    rest = over_components(nyquist * field)
    return field + derive(main) - nyquist * rest


def pack_rows(received):
    lane = lanes()
    inner = jnp.concatenate([received[24 * i : 24 * i + 16] for i in range(NARROW)], axis=0)
    none = jnp.zeros((8, N), F32)
    outer = []
    for i in range(NARROW):
        outer.extend([received[24 * i + 16 : 24 * i + 24], none])
    inner = swap_blocks(inner)
    outer = swap_blocks(jnp.concatenate(outer, axis=0))
    full = jnp.where(lane < 96, inner, 0.0)
    for k in range(2):
        for c in range(3):
            place = 96 + 8 * k + 2 * c
            here = jnp.logical_and(lane >= place, lane < place + 2)
            full = jnp.where(here, roll(outer, place - 16 * (3 * k + c)), full)
    return full


def taps(field, high_ref, low_ref):
    for dz in range(3):
        moved = field if dz == 1 else roll(field, 1 - dz)
        for ref, part in zip((high_ref, low_ref), split(moved)):
            for dy in range(3):
                at = (3 * dy + dz) * 16
                for y in range(16):
                    ref[at : at + 16, N * y : N * y + N] = part[16 * (y + dy) : 16 * (y + dy) + 16]


def shift_rows(value, by):
    return pltpu.roll(value, by % value.shape[0], 0)


def kernel(
    cot, vel, table, index, kcat, tz, ex, ty, tyi, txi, zi, spread, gather,
    out, sums,
    send1, recv1, send2, recv2, send3, recv3, send4, recv4,
    part, recv5, mine, recv6, whole, recv7,
    vext, adv, proj, proj_own, adv_hi, adv_lo, proj_hi, proj_lo,
    hidden, scattered, gpart, gnat, face_x, face_y, corner, gext,
    own_sem, send_sem, recv_sem, vel_send, vel_recv, e1_send, e1_recv, e2_send, e2_recv,
):
    w = lax.axis_index("wide")
    n = lax.axis_index("narrow")
    wy, wz, wx = w // 16, w // 4 % 4, w % 4
    right, left = lax.rem(w + 1, WIDE), lax.rem(w + WIDE - 1, WIDE)
    above, below = lax.rem(n + 1, NARROW), lax.rem(n + NARROW - 1, NARROW)

    def each_wide(act):
        for oz in (2, 1, 3, 0):

            def body(i, carry, oz=oz):
                oy, ox = i // 4, i % 4
                act(lax.rem(wy + oy, 4) * 16 + lax.rem(wz + oz, 4) * 4 + lax.rem(wx + ox, 4))
                return carry

            lax.fori_loop(1 if oz == 0 else 0, 16, body, 0)

    def each_narrow(act):
        def body(i, carry):
            act(lax.rem(n + i, NARROW))
            return carry

        lax.fori_loop(1, NARROW, body, 0)

    barrier = pltpu.get_barrier_semaphore()

    def greet(device):
        pl.semaphore_signal(barrier, inc=1, device_id=device, device_id_type=MESH)

    each_wide(lambda p: greet((p, n)))
    each_narrow(lambda p: greet((w, p)))
    diagonal = ((right, above), (right, below), (left, above), (left, below))
    for device in diagonal:
        greet(device)

    weight = [table[index[l]] for l in range(4)]
    pieces = []
    for x in range(2):
        for c in range(3):
            total = weight[0] * cot[0, c, x]
            for l in range(1, 4):
                total = total + weight[l] * cot[l, c, x]
            pieces.append(total)
    pieces.append(jnp.zeros((32, N), F32))
    combined = jnp.concatenate(pieces, axis=0)
    send1[...] = dot3(both(tz), split(combined), (1, 1))

    pl.semaphore_wait(barrier, WIDE - 1 + NARROW - 1 + 4)

    def exchange(k, axis, rows, source, target):
        size, me = (WIDE, w) if axis == "wide" else (NARROW, n)

        def block(ref, p):
            return ref.at[pl.ds(p * rows, rows)]

        def act(p):
            device = (p, n) if axis == "wide" else (w, p)
            pltpu.make_async_remote_copy(
                source if source.shape[0] == rows else block(source, p),
                block(target, me),
                send_sem.at[k],
                recv_sem.at[k],
                device_id=device,
                device_id_type=MESH,
            ).start()

        (each_wide if axis == "wide" else each_narrow)(act)
        own = pltpu.make_async_copy(
            source if source.shape[0] == rows else block(source, me), block(target, me), own_sem.at[k]
        )
        own.start()
        some = target.at[pl.ds(0, (size - 1) * rows)]
        device = (right, n) if axis == "wide" else (w, above)
        rest = pltpu.make_async_remote_copy(
            some, some, send_sem.at[k], recv_sem.at[k], device_id=device, device_id_type=MESH
        )

        def arrived():
            own.wait()
            rest.wait_recv()

        return arrived, rest.wait_send

    got1, sent1 = exchange(0, "wide", 2, send1, recv1)

    def copies(moves, sends, recvs):
        made = []
        for i, (source, target, device) in enumerate(moves):
            made.append(
                pltpu.make_async_remote_copy(
                    source, target, sends.at[i], recvs.at[i], device_id=device, device_id_type=MESH
                )
            )
        for copy in made:
            copy.start()
        return made

    low, high, full = pl.ds(0, 8), pl.ds(8, 8), pl.ds(0, 16)
    moves = []
    for device, rows, xs, ys in (
        ((right, n), full, 0, pl.ds(8, 16)),
        ((left, n), full, 4, pl.ds(8, 16)),
        ((w, above), high, 2, pl.ds(0, 8)),
        ((w, below), low, 2, pl.ds(24, 8)),
        ((right, above), high, 0, pl.ds(0, 8)),
        ((right, below), low, 0, pl.ds(24, 8)),
        ((left, above), high, 4, pl.ds(0, 8)),
        ((left, below), low, 4, pl.ds(24, 8)),
    ):
        moves.append((vel.at[:, :, rows, :], vext.at[:, pl.ds(xs, 2), ys, :], device))
    vel_copies = copies(moves, vel_send, vel_recv)
    vext[:, 2:4, 8:24, :] = vel[...]

    taps_first = []
    taps_second = []
    for part_of_kernel in split(kcat[...]):
        for place, kind in ((taps_first, 0), (taps_second, 1)):
            rows = part_of_kernel[16 * kind : 16 * kind + 16]
            place.append(
                jnp.concatenate(
                    [dot(rows, spread[kind, x], (1, 0))[:, :144] for x in range(2)], axis=0
                ).astype(BF16)
            )

    proj[...] = jnp.zeros_like(proj)
    gnat[...] = jnp.zeros_like(gnat)
    sublane = lax.broadcasted_iota(jnp.int32, (288, N), 0) % 16
    adv[...] = jnp.where(sublane == 3, 1.0, 0.0)

    for copy in vel_copies:
        copy.wait_recv()
    for x in range(4):
        v = [vext[c, x + 1] for c in range(3)]
        totals = [jnp.zeros((32, N), F32)] * 3
        for j in range(3):
            positive, negative = jnp.maximum(v[j], 0.0), jnp.minimum(v[j], 0.0)
            for c in range(3):
                if j == 0:
                    before, after = vext[c, x], vext[c, x + 2]
                elif j == 1:
                    before, after = shift_rows(v[c], 1), shift_rows(v[c], -1)
                else:
                    before, after = roll(v[c], 1), roll(v[c], -1)
                totals[c] = totals[c] + positive * (v[c] - before) + negative * (after - v[c])
        for c in range(3):
            done = v[c] - STEP * totals[c]
            at = 4 * x + c
            adv[at : at + 1] = done[7:8]
            adv[pl.ds(16 + at, 16, stride=16), :] = done[8:24]
            adv[272 + at : 273 + at] = done[24:25]
    taps(adv[...], adv_hi, adv_lo)
    adv_taps = (adv_hi[...], adv_lo[...])
    hidden[...] = jnp.tanh(dot3(taps_first, adv_taps))

    got1()
    kz_rows = [recv1[pl.ds(k, 64, stride=2), :] for k in range(2)]
    send2[...] = x_transform(kz_rows, both(ex))
    got2, sent2 = exchange(1, "narrow", 16, send2, recv2)

    got2()
    spectrum = dot3(both(ty), split(swap_blocks(recv2[...])))
    spectrum = project(spectrum, w, n)
    send3[...] = dot3(both(tyi), split(spectrum))
    got3, sent3 = exchange(2, "narrow", 24, send3, recv3)

    got3()
    send4[...] = dot3(both(txi), split(pack_rows(recv3[...])))
    got4, sent4 = exchange(3, "wide", 4, send4, recv4)

    got4()
    for x in range(4):
        big = dot3(split(recv4[pl.ds(x, 64, stride=4), :]), both(zi), (0, 0))
        inner = big[:48, :N] + big[48:96, N:]
        outer = big[96:104, :N] + big[104:112, N:]
        for c in range(3):
            at = 4 * x + c
            proj[at : at + 1] = outer[2 * c : 2 * c + 1]
            proj[pl.ds(16 + at, 16, stride=16), :] = inner[16 * c : 16 * c + 16]
            proj[272 + at : 273 + at] = outer[2 * c + 1 : 2 * c + 2]
            if x in (1, 2):
                proj_own[c, x - 1] = inner[16 * c : 16 * c + 16]

    taps(proj[...], proj_hi, proj_lo)
    proj_taps = (proj_hi[...], proj_lo[...])
    hid = hidden[...]
    pre = split(dot3(taps_second, proj_taps) * (1.0 - hid * hid))
    for kind, (rows, cols) in enumerate(((pre, adv_taps), (split(hid), proj_taps))):
        raw = dot3(rows, cols, (1, 1))
        total = jnp.zeros((16, N), F32)
        for x in range(2):
            for piece in split(raw[16 * x : 16 * x + 16]):
                total = total + dot(piece, gather[kind, x], (1, 0))
        part[16 * kind : 16 * kind + 16] = total
    got5, sent5 = exchange(4, "narrow", 4, part, recv5)

    scattered[...] = dot3(taps_first, pre, (0, 0))
    for y in range(18):
        moved = []
        for dz in range(3):
            total = None
            for dy in range(3):
                if 0 <= y - dy < 16:
                    at = (3 * dy + dz) * 16
                    term = scattered[at : at + 16, N * (y - dy) : N * (y - dy) + N]
                    total = term if total is None else total + term
            moved.append(total if dz == 1 else roll(total, dz - 1))
        gpart[16 * y : 16 * y + 16] = moved[0] + moved[1] + moved[2]
    for x in range(4):
        for c in range(3):
            at = 4 * x + c
            gnat[c, x, 7:8] = gpart[at : at + 1]
            gnat[c, x, 8:24] = gpart[pl.ds(16 + at, 16, stride=16), :]
            gnat[c, x, 24:25] = gpart[272 + at : 273 + at]
    own_x, own_y = pl.ds(1, 2), pl.ds(8, 16)
    first_y, last_y = pl.ds(0, 8), pl.ds(24, 8)
    e1 = copies(
        [
            (gnat.at[:, 0, own_y, :], face_x.at[1], (left, n)),
            (gnat.at[:, 3, own_y, :], face_x.at[0], (right, n)),
            (gnat.at[:, own_x, first_y, :], face_y.at[1], (w, below)),
            (gnat.at[:, own_x, last_y, :], face_y.at[0], (w, above)),
            (gnat.at[:, 0, first_y, :], corner.at[3], (left, below)),
            (gnat.at[:, 0, last_y, :], corner.at[2], (left, above)),
            (gnat.at[:, 3, first_y, :], corner.at[1], (right, below)),
            (gnat.at[:, 3, last_y, :], corner.at[0], (right, above)),
        ],
        e1_send,
        e1_recv,
    )

    got5()

    def fold(value):
        value = jnp.sum(value.reshape(value.shape[0] // 8, 8, N), axis=0)
        return value[0:4] + value[4:8]

    mine[...] = fold(recv5[...])
    got6, sent6 = exchange(5, "wide", 4, mine, recv6)

    for copy in e1:
        copy.wait_recv()
    for c in range(3):
        for x in range(2):
            own = proj_own[c, x] + gnat[c, x + 1, 8:24] + face_x[x, c]
            start = own[0:8] + face_y[0, c, x] + corner[2 * x, c]
            end = own[8:16] + face_y[1, c, x] + corner[2 * x + 1, c]
            gext[c, x + 1, 8:16] = start
            gext[c, x + 1, 16:24] = end
    e2 = copies(
        [
            (gext.at[:, 1, own_y, :], gext.at[:, 3, own_y, :], (left, n)),
            (gext.at[:, 2, own_y, :], gext.at[:, 0, own_y, :], (right, n)),
            (gext.at[:, own_x, pl.ds(8, 8), :], gext.at[:, own_x, last_y, :], (w, below)),
            (gext.at[:, own_x, pl.ds(16, 8), :], gext.at[:, own_x, first_y, :], (w, above)),
        ],
        e2_send,
        e2_recv,
    )
    for copy in e2:
        copy.wait_recv()

    for x in range(2):
        vx, gx = x + 2, x + 1
        v = [vext[c, vx] for c in range(3)]
        g = [gext[c, gx] for c in range(3)]
        positive = [jnp.maximum(a, 0.0) for a in v]
        negative = [jnp.minimum(a, 0.0) for a in v]
        totals = [jnp.zeros((32, N), F32)] * 3
        slopes = []
        for j in range(3):
            slope = jnp.zeros((32, N), F32)
            for c in range(3):
                here = (positive[j] - negative[j]) * g[c]
                if j == 0:
                    ahead = jnp.maximum(vext[0, vx + 1], 0.0) * gext[c, gx + 1]
                    behind = jnp.minimum(vext[0, vx - 1], 0.0) * gext[c, gx - 1]
                    before, after = vext[c, vx - 1], vext[c, vx + 1]
                elif j == 1:
                    ahead = shift_rows(positive[1] * g[c], -1)
                    behind = shift_rows(negative[1] * g[c], 1)
                    before, after = shift_rows(v[c], 1), shift_rows(v[c], -1)
                else:
                    ahead = roll(positive[2] * g[c], -1)
                    behind = roll(negative[2] * g[c], 1)
                    before, after = roll(v[c], 1), roll(v[c], -1)
                totals[c] = totals[c] + here - ahead + behind
                rising, falling = v[c] - before, after - v[c]
                level = 0.5 * (rising + falling)
                slope = slope + g[c] * jnp.where(
                    v[j] > 0.0, rising, jnp.where(v[j] < 0.0, falling, level)
                )
            slopes.append(slope)
        for c in range(3):
            out[c, x] = (g[c] - STEP * totals[c] - STEP * slopes[c])[8:24]

    got6()
    whole[...] = fold(recv6[...]) * (N * N * N) ** -0.5
    got7, sent7 = exchange(6, "narrow", 4, whole, recv7)
    got7()
    sums[...] = recv7[...]

    for sent in (sent1, sent2, sent3, sent4, sent5, sent6, sent7):
        sent()
    for copy in vel_copies + e1 + e2:
        copy.wait_send()


def local(velocity, cotangents, lead_table, lead_index, first_kernel, first_bias, second_kernel):
    first = jnp.concatenate([first_kernel.reshape(16, 81), first_bias[:, None]], axis=1)
    second = jnp.transpose(second_kernel.reshape(3, 16, 27), (1, 0, 2)).reshape(16, 81)
    kcat = jnp.concatenate(
        [jnp.pad(first, ((0, 0), (0, N - 82))), jnp.pad(second, ((0, 0), (0, N - 81)))], axis=0
    )
    constants = [jnp.asarray(t) for t in tables()]

    def v(*shape, kind=F32):
        return pltpu.VMEM(shape, kind)

    dma = pltpu.SemaphoreType.DMA
    in_vmem = pl.BlockSpec(memory_space=pltpu.VMEM)
    in_smem = pl.BlockSpec(memory_space=pltpu.SMEM)
    grad, sums = pl.pallas_call(
        kernel,
        out_shape=(
            jax.ShapeDtypeStruct((3, 2, 16, N), F32),
            jax.ShapeDtypeStruct((32, N), F32),
        ),
        in_specs=[in_vmem, in_vmem, in_smem, in_smem, in_vmem] + [in_vmem] * len(constants),
        out_specs=(in_vmem, in_vmem),
        scratch_shapes=[
            v(128, N), v(128, N), v(128, N), v(128, N), v(192, N), v(192, N), v(256, N), v(256, N),
            v(32, N), v(32, N), v(4, N), v(256, N), v(4, N), v(32, N),
            v(3, 6, 32, N), v(288, N), v(288, N), v(3, 2, 16, N),
            v(144, 2048, kind=BF16), v(144, 2048, kind=BF16),
            v(144, 2048, kind=BF16), v(144, 2048, kind=BF16),
            v(32, 2048), v(144, 2048), v(288, N), v(3, 4, 32, N),
            v(2, 3, 16, N), v(2, 3, 2, 8, N), v(4, 3, 8, N), v(3, 4, 32, N),
            dma((7,)), dma((7,)), dma((7,)), dma((8,)), dma((8,)), dma((8,)), dma((8,)),
            dma((4,)), dma((4,)),
        ],
        compiler_params=pltpu.CompilerParams(
            collective_id=0, has_side_effects=True, vmem_limit_bytes=48 * 1024 * 1024
        ),
        name="step_backward",
    )(cotangents, velocity, lead_table, lead_index, kcat, *constants)
    grad_first = sums[:16, :81].reshape(16, 3, 3, 3, 3)
    grad_bias = sums[:16, 81]
    grad_second = jnp.transpose(sums[16:, :81].reshape(16, 3, 27), (1, 0, 2)).reshape(3, 16, 3, 3, 3)
    return grad, grad_first, grad_bias, grad_second


def solution(mesh):
    placed = (
        P(None, "wide", "narrow", None),
        P(None, None, "wide", "narrow", None),
        P(),
        P(),
        P(),
        P(),
        P(),
    )
    return jax.shard_map(
        local,
        mesh=mesh,
        in_specs=placed,
        out_specs=(P(None, "wide", "narrow", None), P(), P(), P()),
        check_vma=False,
    )
```

profile of v0, /device:TPU:1, one launch (start us, length us, event | category | flops | bytes accessed | tf_op | source)
XLA Modules:
  0.0 101.3 jit_solution(15831559345343740125)
XLA Ops:
  0.6 0.0 copy-start
  0.6 0.8 copy.25
  1.4 0.0 copy-start.1
  1.4 0.9 reshape.26
  2.3 0.1 copy.24
  2.4 0.1 select_maximum_fusion.1
  2.4 0.8 reshape.27
  3.3 0.1 copy.26
  3.4 0.1 reshape.28
  3.5 0.0 copy-start.10
  3.5 0.0 copy-start.11
  3.5 0.0 copy-done
  3.5 0.0 copy-done.1
  3.5 0.6 copy-done.10
  4.1 0.0 copy-done.11
  4.1 0.0 copy-start.2
  4.1 0.9 copy-done.2
  5.1 0.0 copy-start.3
  5.1 0.9 copy-done.3
  6.0 0.0 copy-start.4
  6.0 0.9 copy-done.4
  6.9 0.0 copy-start.5
  6.9 0.9 copy-done.5
  7.8 0.0 copy-start.6
  7.8 0.8 copy-done.6
  8.6 0.0 copy-start.7
  8.6 0.8 copy-done.7
  9.4 0.0 copy-start.8
  9.4 0.8 copy-done.8
  10.3 0.0 copy-start.9
  10.3 0.8 copy-done.9
  11.1 87.3 %step_backward.1 = (f32[3,2,16,128]{3,2,1,0:T(8,128)S(1)}, f32[32,128]{1,0:T(8,128)S(1)}) custom-call(f32[4,3,2,16,128]{4,3,2,1,0:T(8,128)S(1)} %copy-done.1, f32[3,2,16,128]{3,2,1,0:T(8,128)S(1)} %copy-done.9, f32[8]{0:T(128)S(1)} %copy-done.10, s32[4]{0:T(128)S(1)} %copy-done.11, f32[32,128]{1,0:T(8,128)S(1)} %select_maximum_fusion.kcat, ...), custom_call_target="tpu_custom_call" | custom-call | tf_op jit(solution)/shard_map/step_backward/pallas_call | solution.py:534
  98.4 0.7 slice_reduce_fusion
  99.1 0.1 reshape.30
  99.2 0.1 copy.28
  99.3 0.7 reshape.31
  99.9 0.1 copy.27
  100.0 0.6 reshape.29
  100.7 0.6 copy.30
  (2 shorter events, 0.0 us)
Async XLA Ops:
  0.6 2.9 %copy-start = (bf16[2,2,128,256]{3,2,1,0:T(8,128)(2,1)S(1)}, bf16[2,2,128,256]{3,2,1,0:T(8,128)(2,1)}, u32[]{:S(2)}) copy-start(bf16[2,2,128,256]{3,2,1,0:T(8,128)(2,1)} %constant.25.clone.spread) | copy-start | bytes 786436
  1.4 2.1 %copy-start.1 = (f32[4,3,2,16,128]{4,3,2,1,0:T(8,128)S(1)}, f32[4,3,2,16,128]{4,3,2,1,0:T(8,128)}, u32[]{:S(2)}) copy-start(f32[4,3,2,16,128]{4,3,2,1,0:T(8,128)} %cot.1) | copy-start | bytes 589828
  3.5 0.7 copy-start.10
  3.5 0.7 copy-start.11
  4.1 0.9 copy-start.2
  5.1 0.9 copy-start.3
  6.0 0.9 copy-start.4
  6.9 0.9 copy-start.5
  7.8 0.8 copy-start.6
  8.6 0.8 copy-start.7
  9.4 0.8 copy-start.8
  10.3 0.8 copy-start.9
where the time goes:
time: 102 us; the launch traced here: 101 us
  Pallas kernels  87.3 us (86%)
  local copies, waits for them, and re-layouts  13.2 us (13%)
    pallas_call x1, Pallas kernels, local(): pl.pallas_call(kernel, out_shape=(jax.ShapeDtypeStruct((3, 2, 16, N), F32...  87.3 us
    unnamed x25, local copies, waits for them, and re-layouts  8.2 us

commit v1 on v0

--- a/solution.py
+++ b/solution.py
@@ -16,6 +16,8 @@
 WIDE = 64
 NARROW = 8
 STEP = 0.25
+BIAS = 108
+TABLES = 8
 
 
 def basis(kind, wave):
@@ -47,7 +49,7 @@
         rows.extend([np.zeros(N)] * 6)
     tyi = np.stack(rows)
     txi = np.stack([tx[:, (2 * w - 1 + x) % N] for w in range(WIDE) for x in range(4)])
-    zi = np.concatenate([tz[0::2], tz[1::2]], axis=1)
+    zi = np.stack([tz[0::2], tz[1::2]])
     spread = np.zeros((2, 2, N, 256))
     gather = np.zeros((2, 2, 144, N))
     for x in range(2):
@@ -55,15 +57,15 @@
             for dx in range(3):
                 for dy in range(3):
                     for dz in range(3):
-                        flat = c * 27 + dx * 9 + dy * 3 + dz
+                        flat = 4 * (c * 9 + dx * 3 + dy) + dz
                         lane = (dy * 3 + dz) * 16 + 4 * (x + dx) + c
                         back = ((2 - dy) * 3 + 2 - dz) * 16 + 4 * (x + 2 - dx) + c
                         spread[0, x, flat, lane] = 1.0
                         spread[1, x, flat, back] = 1.0
                         gather[0, x, lane, flat] = 1.0
                         gather[1, x, back, flat] = 1.0
-        spread[0, x, 81, 4 * 16 + 3] = 1.0
-        gather[0, x, 4 * 16 + 3, 81] = 1.0
+        spread[0, x, BIAS, 4 * 16 + 3] = 1.0
+        gather[0, x, 4 * 16 + 3, BIAS] = 1.0
     exact = ml_dtypes.bfloat16
     return (
         halves(tz),
@@ -72,7 +74,7 @@
         halves(tyi),
         halves(txi),
         halves(zi),
-        spread.astype(exact),
+        np.stack([spread[..., :N], spread[..., N:]], axis=2).astype(exact),
         gather.astype(exact),
     )
 
@@ -203,48 +205,109 @@
 
 
 def kernel(
-    cot, vel, table, index, kcat, tz, ex, ty, tyi, txi, zi, spread, gather,
-    out, sums,
+    cot_hbm, vel_hbm, table_hbm, index_hbm, first_hbm, bias_hbm, second_hbm, *refs
+):
+    tables_hbm, refs = refs[:TABLES], refs[TABLES:]
+    (out, sums), refs = refs[:2], refs[2:]
+    (cot, table, index, first, bias, second), refs = refs[:6], refs[6:]
+    (tz, ex, ty, tyi, txi, zi, spread, gather), refs = refs[:TABLES], refs[TABLES:]
+    (
     send1, recv1, send2, recv2, send3, recv3, send4, recv4,
     part, recv5, mine, recv6, whole, recv7,
     vext, adv, proj, proj_own, adv_hi, adv_lo, proj_hi, proj_lo,
     hidden, scattered, gpart, gnat, face_x, face_y, corner, gext,
-    own_sem, send_sem, recv_sem, vel_send, vel_recv, e1_send, e1_recv, e2_send, e2_recv,
-):
+    flat, own_sem, send_sem, recv_sem, vel_send, vel_recv, e1_send, e1_recv, e2_send, e2_recv,
+    load_sem,
+    ) = refs
     w = lax.axis_index("wide")
     n = lax.axis_index("narrow")
     wy, wz, wx = w // 16, w // 4 % 4, w % 4
+    zl, core = n // 2, n % 2
     right, left = lax.rem(w + 1, WIDE), lax.rem(w + WIDE - 1, WIDE)
     above, below = lax.rem(n + 1, NARROW), lax.rem(n + NARROW - 1, NARROW)
 
+    column = 16 * wy + 4 * wz + zl
+    member = 2 * wx + core
+    stays = wx == zl
+
+    def each_column(act):
+        def body(i, carry):
+            j = i // 4
+            oz = 8 + jnp.where(j % 2 == 1, (j + 1) // 2, -(j // 2))
+            act(lax.rem(wy + 3 - i % 4, 4) * 16 + lax.rem(4 * wz + zl + oz, 16))
+            return carry
+
+        lax.fori_loop(0, WIDE - 1, body, 0)
+
     def each_wide(act):
         for oz in (2, 1, 3, 0):
 
             def body(i, carry, oz=oz):
-                oy, ox = i // 4, i % 4
-                act(lax.rem(wy + oy, 4) * 16 + lax.rem(wz + oz, 4) * 4 + lax.rem(wx + ox, 4))
+                y, x = lax.rem(wy + 3 - i // 4, 4), lax.rem(wx + 3 - i % 4, 4)
+                act(y * 16 + lax.rem(wz + oz, 4) * 4 + x)
                 return carry
 
-            lax.fori_loop(1 if oz == 0 else 0, 16, body, 0)
-
-    def each_narrow(act):
-        def body(i, carry):
-            act(lax.rem(n + i, NARROW))
-            return carry
-
-        lax.fori_loop(1, NARROW, body, 0)
+            lax.fori_loop(0, 15 if oz == 0 else 16, body, 0)
+
+    def each_member(act):
+        for i in (4, 5, 3, 2, 6, 7, 1):
+            act(lax.rem(member + i, NARROW))
+
+    def at_column(p, x):
+        return (p // 16 * 16 + p % 16 // 4 * 4 + x, p % 4 * 2 + core)
+
+    outward = (WIDE, each_column, lambda p: at_column(p, zl), column, w, stays)
+    inward = (WIDE, each_wide, lambda p: (p, member), w, column, stays)
+    columns = (WIDE, each_column, lambda p: at_column(p, wx), column, column, None)
+    members = (
+        NARROW,
+        each_member,
+        lambda p: (w - wx + p // 2, n - core + p % 2),
+        member,
+        member,
+        None,
+    )
 
     barrier = pltpu.get_barrier_semaphore()
 
     def greet(device):
         pl.semaphore_signal(barrier, inc=1, device_id=device, device_id_type=MESH)
 
-    each_wide(lambda p: greet((p, n)))
-    each_narrow(lambda p: greet((w, p)))
-    diagonal = ((right, above), (right, below), (left, above), (left, below))
-    for device in diagonal:
+    each_wide(lambda p: greet((p, member)))
+
+    @pl.when(jnp.logical_not(stays))
+    def _():
+        greet((w, member))
+
+    each_member(lambda p: greet(members[2](p)))
+    neighbours = (
+        (right, n), (left, n), (w, above), (w, below),
+        (right, above), (right, below), (left, above), (left, below),
+    )
+    for device in neighbours:
         greet(device)
 
+    loads = [
+        pltpu.make_async_copy(source, target, load_sem.at[i])
+        for i, (source, target) in enumerate(
+            [
+                (cot_hbm, cot),
+                (table_hbm, table),
+                (index_hbm, index),
+                (tables_hbm[0], tz),
+                (vel_hbm, vext.at[:, pl.ds(2, 2), pl.ds(8, 16), :]),
+                (first_hbm, first),
+                (bias_hbm, bias),
+                (second_hbm, second),
+            ]
+            + list(zip(tables_hbm[1:], (ex, ty, tyi, txi, zi, spread, gather)))
+        )
+    ]
+    for load in loads:
+        load.start()
+
+    for load in loads[:4]:
+        load.wait()
     weight = [table[index[l]] for l in range(4)]
     pieces = []
     for x in range(2):
@@ -257,43 +320,31 @@
     combined = jnp.concatenate(pieces, axis=0)
     send1[...] = dot3(both(tz), split(combined), (1, 1))
 
-    pl.semaphore_wait(barrier, WIDE - 1 + NARROW - 1 + 4)
-
-    def exchange(k, axis, rows, source, target):
-        size, me = (WIDE, w) if axis == "wide" else (NARROW, n)
-
-        def block(ref, p):
-            return ref.at[pl.ds(p * rows, rows)]
-
-        def act(p):
-            device = (p, n) if axis == "wide" else (w, p)
-            pltpu.make_async_remote_copy(
-                source if source.shape[0] == rows else block(source, p),
-                block(target, me),
-                send_sem.at[k],
-                recv_sem.at[k],
-                device_id=device,
-                device_id_type=MESH,
-            ).start()
-
-        (each_wide if axis == "wide" else each_narrow)(act)
-        own = pltpu.make_async_copy(
-            source if source.shape[0] == rows else block(source, me), block(target, me), own_sem.at[k]
-        )
-        own.start()
-        some = target.at[pl.ds(0, (size - 1) * rows)]
-        device = (right, n) if axis == "wide" else (w, above)
-        rest = pltpu.make_async_remote_copy(
-            some, some, send_sem.at[k], recv_sem.at[k], device_id=device, device_id_type=MESH
-        )
-
-        def arrived():
-            own.wait()
-            rest.wait_recv()
-
-        return arrived, rest.wait_send
-
-    got1, sent1 = exchange(0, "wide", 2, send1, recv1)
+    for load in loads[4:]:
+        load.wait()
+
+    taps_first, taps_second = [], []
+    for kind, (ref, place) in enumerate(((first, taps_first), (second, taps_second))):
+        flat[...] = jnp.zeros_like(flat)
+        for tap in range(27):
+            flat[4 * tap : 4 * tap + 3, 0:16] = ref[tap // 9, tap // 3 % 3, tap % 3]
+        if kind == 0:
+            flat[BIAS : BIAS + 1, 0:16] = bias[...]
+        for piece in split(flat[...]):
+            rows = []
+            for x in range(2):
+                cols = [dot(piece, spread[kind, x, i], (0, 0))[:16] for i in range(2)]
+                rows.append(jnp.concatenate(cols, axis=1)[:, :144])
+            place.append(jnp.concatenate(rows, axis=0).astype(BF16))
+
+    proj[...] = jnp.zeros_like(proj)
+    face_y[...] = jnp.zeros_like(face_y)
+    corner[...] = jnp.zeros_like(corner)
+    sublane = lax.broadcasted_iota(jnp.int32, (288, N), 0) % 16
+    adv[...] = jnp.where(sublane == 3, 1.0, 0.0)
+
+    pl.semaphore_wait(barrier, WIDE + NARROW + 6 + jnp.where(stays, 0, 1))
+    pending = []
 
     def copies(moves, sends, recvs):
         made = []
@@ -305,39 +356,85 @@
             )
         for copy in made:
             copy.start()
+            pending.append(copy.wait_send)
         return made
 
-    low, high, full = pl.ds(0, 8), pl.ds(8, 8), pl.ds(0, 16)
+    def exchange(i, group, rows, source, target):
+        size, each, device, own, slot, kept = group
+
+        def block(ref, p):
+            return ref.at[pl.ds(p * rows, rows)]
+
+        def piece(p):
+            return source if source.shape[0] == rows else block(source, p)
+
+        def copy(a, b, to):
+            return pltpu.make_async_remote_copy(
+                a, b, send_sem.at[i], recv_sem.at[i], device_id=to, device_id_type=MESH
+            )
+
+        def act(p):
+            copy(piece(p), block(target, slot), device(p)).start()
+
+        each(act)
+        keep = pltpu.make_async_copy(piece(own), block(target, slot), own_sem.at[i])
+        some = target.at[pl.ds(0, (size - 1) * rows)]
+        others = copy(some, some, (right, n))
+        if kept is None:
+            keep.start()
+            pending.append(others.wait_send)
+
+            def arrived():
+                keep.wait()
+                others.wait_recv()
+
+            return arrived
+        everyone = copy(target, target, (right, n))
+
+        def either(here, there):
+            pl.when(kept)(here)
+            pl.when(jnp.logical_not(kept))(there)
+
+        either(lambda: keep.start(), lambda: act(own))
+        pending.append(lambda: either(lambda: others.wait_send(), lambda: everyone.wait_send()))
+
+        def arrived():
+            def here():
+                keep.wait()
+                others.wait_recv()
+
+            either(here, lambda: everyone.wait_recv())
+
+        return arrived
+
+    got1 = exchange(0, outward, 2, send1, recv1)
+
+    got1()
+    kz_rows = [recv1[pl.ds(k, 64, stride=2), :] for k in range(2)]
+    send2[...] = x_transform(kz_rows, both(ex))
+    got2 = exchange(1, members, 16, send2, recv2)
+
+    low, high, full = pl.ds(8, 2), pl.ds(22, 2), pl.ds(8, 16)
     moves = []
-    for device, rows, xs, ys in (
-        ((right, n), full, 0, pl.ds(8, 16)),
-        ((left, n), full, 4, pl.ds(8, 16)),
-        ((w, above), high, 2, pl.ds(0, 8)),
-        ((w, below), low, 2, pl.ds(24, 8)),
-        ((right, above), high, 0, pl.ds(0, 8)),
-        ((right, below), low, 0, pl.ds(24, 8)),
-        ((left, above), high, 4, pl.ds(0, 8)),
-        ((left, below), low, 4, pl.ds(24, 8)),
+    for device, rows, xs, ys in zip(
+        neighbours,
+        (full, full, high, low, high, low, high, low),
+        (0, 4, 2, 2, 0, 0, 4, 4),
+        (full, full, pl.ds(6, 2), pl.ds(24, 2)) + (pl.ds(6, 2), pl.ds(24, 2)) * 2,
     ):
-        moves.append((vel.at[:, :, rows, :], vext.at[:, pl.ds(xs, 2), ys, :], device))
+        source = vext.at[:, pl.ds(2, 2), rows, :]
+        moves.append((source, vext.at[:, pl.ds(xs, 2), ys, :], device))
     vel_copies = copies(moves, vel_send, vel_recv)
-    vext[:, 2:4, 8:24, :] = vel[...]
-
-    taps_first = []
-    taps_second = []
-    for part_of_kernel in split(kcat[...]):
-        for place, kind in ((taps_first, 0), (taps_second, 1)):
-            rows = part_of_kernel[16 * kind : 16 * kind + 16]
-            place.append(
-                jnp.concatenate(
-                    [dot(rows, spread[kind, x], (1, 0))[:, :144] for x in range(2)], axis=0
-                ).astype(BF16)
-            )
-
-    proj[...] = jnp.zeros_like(proj)
-    gnat[...] = jnp.zeros_like(gnat)
-    sublane = lax.broadcasted_iota(jnp.int32, (288, N), 0) % 16
-    adv[...] = jnp.where(sublane == 3, 1.0, 0.0)
+
+    got2()
+    spectrum = dot3(both(ty), split(swap_blocks(recv2[...])))
+    spectrum = project(spectrum, column, member)
+    send3[...] = dot3(both(tyi), split(spectrum))
+    got3 = exchange(2, members, 24, send3, recv3)
+
+    got3()
+    send4[...] = dot3(both(txi), split(pack_rows(recv3[...])))
+    got4 = exchange(3, inward, 4, send4, recv4)
 
     for copy in vel_copies:
         copy.wait_recv()
@@ -364,26 +461,12 @@
     adv_taps = (adv_hi[...], adv_lo[...])
     hidden[...] = jnp.tanh(dot3(taps_first, adv_taps))
 
-    got1()
-    kz_rows = [recv1[pl.ds(k, 64, stride=2), :] for k in range(2)]
-    send2[...] = x_transform(kz_rows, both(ex))
-    got2, sent2 = exchange(1, "narrow", 16, send2, recv2)
-
-    got2()
-    spectrum = dot3(both(ty), split(swap_blocks(recv2[...])))
-    spectrum = project(spectrum, w, n)
-    send3[...] = dot3(both(tyi), split(spectrum))
-    got3, sent3 = exchange(2, "narrow", 24, send3, recv3)
-
-    got3()
-    send4[...] = dot3(both(txi), split(pack_rows(recv3[...])))
-    got4, sent4 = exchange(3, "wide", 4, send4, recv4)
-
     got4()
     for x in range(4):
-        big = dot3(split(recv4[pl.ds(x, 64, stride=4), :]), both(zi), (0, 0))
-        inner = big[:48, :N] + big[48:96, N:]
-        outer = big[96:104, :N] + big[104:112, N:]
+        rows = split(recv4[pl.ds(x, 64, stride=4), :])
+        even, odd = (dot3(rows, (zi[0, k], zi[1, k]), (0, 0)) for k in range(2))
+        inner = even[:48] + odd[48:96]
+        outer = even[96:104] + odd[104:112]
         for c in range(3):
             at = 4 * x + c
             proj[at : at + 1] = outer[2 * c : 2 * c + 1]
@@ -396,14 +479,6 @@
     proj_taps = (proj_hi[...], proj_lo[...])
     hid = hidden[...]
     pre = split(dot3(taps_second, proj_taps) * (1.0 - hid * hid))
-    for kind, (rows, cols) in enumerate(((pre, adv_taps), (split(hid), proj_taps))):
-        raw = dot3(rows, cols, (1, 1))
-        total = jnp.zeros((16, N), F32)
-        for x in range(2):
-            for piece in split(raw[16 * x : 16 * x + 16]):
-                total = total + dot(piece, gather[kind, x], (1, 0))
-        part[16 * kind : 16 * kind + 16] = total
-    got5, sent5 = exchange(4, "narrow", 4, part, recv5)
 
     scattered[...] = dot3(taps_first, pre, (0, 0))
     for y in range(18):
@@ -424,22 +499,31 @@
             gnat[c, x, 8:24] = gpart[pl.ds(16 + at, 16, stride=16), :]
             gnat[c, x, 24:25] = gpart[272 + at : 273 + at]
     own_x, own_y = pl.ds(1, 2), pl.ds(8, 16)
-    first_y, last_y = pl.ds(0, 8), pl.ds(24, 8)
+    row_0, row_7, row_8, row_23, row_24 = (pl.ds(r, 1) for r in (0, 7, 8, 23, 24))
     e1 = copies(
         [
+            (gnat.at[:, 3, own_y, :], face_x.at[0], (right, n)),
             (gnat.at[:, 0, own_y, :], face_x.at[1], (left, n)),
-            (gnat.at[:, 3, own_y, :], face_x.at[0], (right, n)),
-            (gnat.at[:, own_x, first_y, :], face_y.at[1], (w, below)),
-            (gnat.at[:, own_x, last_y, :], face_y.at[0], (w, above)),
-            (gnat.at[:, 0, first_y, :], corner.at[3], (left, below)),
-            (gnat.at[:, 0, last_y, :], corner.at[2], (left, above)),
-            (gnat.at[:, 3, first_y, :], corner.at[1], (right, below)),
-            (gnat.at[:, 3, last_y, :], corner.at[0], (right, above)),
+            (gnat.at[:, own_x, row_24, :], face_y.at[0, :, :, row_0, :], (w, above)),
+            (gnat.at[:, own_x, row_7, :], face_y.at[1, :, :, row_7, :], (w, below)),
+            (gnat.at[:, 3, row_24, :], corner.at[0, :, row_0, :], (right, above)),
+            (gnat.at[:, 3, row_7, :], corner.at[1, :, row_7, :], (right, below)),
+            (gnat.at[:, 0, row_24, :], corner.at[2, :, row_0, :], (left, above)),
+            (gnat.at[:, 0, row_7, :], corner.at[3, :, row_7, :], (left, below)),
         ],
         e1_send,
         e1_recv,
     )
 
+    for kind, (rows, cols) in enumerate(((pre, adv_taps), (split(hid), proj_taps))):
+        raw = dot3(rows, cols, (1, 1))
+        total = jnp.zeros((16, N), F32)
+        for x in range(2):
+            for piece in split(raw[16 * x : 16 * x + 16]):
+                total = total + dot(piece, gather[kind, x], (1, 0))
+        part[16 * kind : 16 * kind + 16] = total
+    got5 = exchange(4, members, 4, part, recv5)
+
     got5()
 
     def fold(value):
@@ -447,7 +531,7 @@
         return value[0:4] + value[4:8]
 
     mine[...] = fold(recv5[...])
-    got6, sent6 = exchange(5, "wide", 4, mine, recv6)
+    got6 = exchange(5, columns, 4, mine, recv6)
 
     for copy in e1:
         copy.wait_recv()
@@ -462,12 +546,16 @@
         [
             (gext.at[:, 1, own_y, :], gext.at[:, 3, own_y, :], (left, n)),
             (gext.at[:, 2, own_y, :], gext.at[:, 0, own_y, :], (right, n)),
-            (gext.at[:, own_x, pl.ds(8, 8), :], gext.at[:, own_x, last_y, :], (w, below)),
-            (gext.at[:, own_x, pl.ds(16, 8), :], gext.at[:, own_x, first_y, :], (w, above)),
+            (gext.at[:, own_x, row_8, :], gext.at[:, own_x, row_24, :], (w, below)),
+            (gext.at[:, own_x, row_23, :], gext.at[:, own_x, row_7, :], (w, above)),
         ],
         e2_send,
         e2_recv,
     )
+    got6()
+    whole[...] = fold(recv6[...]) * (N * N * N) ** -0.5
+    got7 = exchange(6, members, 4, whole, recv7)
+
     for copy in e2:
         copy.wait_recv()
 
@@ -505,41 +593,45 @@
         for c in range(3):
             out[c, x] = (g[c] - STEP * totals[c] - STEP * slopes[c])[8:24]
 
-    got6()
-    whole[...] = fold(recv6[...]) * (N * N * N) ** -0.5
-    got7, sent7 = exchange(6, "narrow", 4, whole, recv7)
     got7()
     sums[...] = recv7[...]
 
-    for sent in (sent1, sent2, sent3, sent4, sent5, sent6, sent7):
-        sent()
-    for copy in vel_copies + e1 + e2:
-        copy.wait_send()
+    for wait in pending:
+        wait()
+
+
+def hand_out(grad, sums, out, out_first, out_bias, out_second):
+    out[...] = grad[...]
+    for kind, ref in enumerate((out_first, out_second)):
+        turned = sums[16 * kind : 16 * kind + 16].T
+        for tap in range(27):
+            ref[tap // 9, tap // 3 % 3, tap % 3] = turned[4 * tap : 4 * tap + 3]
+        if kind == 0:
+            out_bias[...] = turned[BIAS : BIAS + 1]
 
 
 def local(velocity, cotangents, lead_table, lead_index, first_kernel, first_bias, second_kernel):
-    first = jnp.concatenate([first_kernel.reshape(16, 81), first_bias[:, None]], axis=1)
-    second = jnp.transpose(second_kernel.reshape(3, 16, 27), (1, 0, 2)).reshape(16, 81)
-    kcat = jnp.concatenate(
-        [jnp.pad(first, ((0, 0), (0, N - 82))), jnp.pad(second, ((0, 0), (0, N - 81)))], axis=0
-    )
-    constants = [jnp.asarray(t) for t in tables()]
+    constants = tables()
 
     def v(*shape, kind=F32):
         return pltpu.VMEM(shape, kind)
 
     dma = pltpu.SemaphoreType.DMA
     in_vmem = pl.BlockSpec(memory_space=pltpu.VMEM)
-    in_smem = pl.BlockSpec(memory_space=pltpu.SMEM)
-    grad, sums = pl.pallas_call(
+    anywhere = pl.BlockSpec(memory_space=pl.ANY)
+    shapes = tuple(
+        jax.ShapeDtypeStruct(shape, F32)
+        for shape in ((3, 2, 16, N), (3, 3, 3, 3, 16), (1, 16), (3, 3, 3, 3, 16))
+    )
+    results = pl.pallas_call(
         kernel,
-        out_shape=(
-            jax.ShapeDtypeStruct((3, 2, 16, N), F32),
-            jax.ShapeDtypeStruct((32, N), F32),
-        ),
-        in_specs=[in_vmem, in_vmem, in_smem, in_smem, in_vmem] + [in_vmem] * len(constants),
-        out_specs=(in_vmem, in_vmem),
+        out_shape=(shapes[0], jax.ShapeDtypeStruct((32, N), F32)),
+        in_specs=[anywhere] * (7 + TABLES),
+        out_specs=(in_vmem,) * 2,
         scratch_shapes=[
+            v(4, 3, 2, 16, N), pltpu.SMEM((8,), F32), pltpu.SMEM((4,), jnp.int32),
+            v(3, 3, 3, 3, 16), v(1, 16), v(3, 3, 3, 3, 16),
+            *[v(*t.shape, kind=BF16) for t in constants],
             v(128, N), v(128, N), v(128, N), v(128, N), v(192, N), v(192, N), v(256, N), v(256, N),
             v(32, N), v(32, N), v(4, N), v(256, N), v(4, N), v(32, N),
             v(3, 6, 32, N), v(288, N), v(288, N), v(3, 2, 16, N),
@@ -547,18 +639,31 @@
             v(144, 2048, kind=BF16), v(144, 2048, kind=BF16),
             v(32, 2048), v(144, 2048), v(288, N), v(3, 4, 32, N),
             v(2, 3, 16, N), v(2, 3, 2, 8, N), v(4, 3, 8, N), v(3, 4, 32, N),
-            dma((7,)), dma((7,)), dma((7,)), dma((8,)), dma((8,)), dma((8,)), dma((8,)),
-            dma((4,)), dma((4,)),
+            v(N, N), dma((7,)), dma((7,)), dma((7,)), dma((8,)), dma((8,)), dma((8,)), dma((8,)),
+            dma((4,)), dma((4,)), dma((7 + TABLES,)),
         ],
         compiler_params=pltpu.CompilerParams(
-            collective_id=0, has_side_effects=True, vmem_limit_bytes=48 * 1024 * 1024
+            collective_id=0, has_side_effects=True, vmem_limit_bytes=60 * 1024 * 1024
         ),
         name="step_backward",
-    )(cotangents, velocity, lead_table, lead_index, kcat, *constants)
-    grad_first = sums[:16, :81].reshape(16, 3, 3, 3, 3)
-    grad_bias = sums[:16, 81]
-    grad_second = jnp.transpose(sums[16:, :81].reshape(16, 3, 27), (1, 0, 2)).reshape(3, 16, 3, 3, 3)
-    return grad, grad_first, grad_bias, grad_second
+    )(
+        cotangents, velocity, lead_table, lead_index,
+        jnp.transpose(first_kernel, (1, 2, 3, 4, 0)), first_bias[None],
+        jnp.transpose(second_kernel, (0, 2, 3, 4, 1)), *[jnp.asarray(t) for t in constants],
+    )
+    grad, first, bias, second = pl.pallas_call(
+        hand_out,
+        out_shape=shapes,
+        in_specs=[in_vmem] * 2,
+        out_specs=(in_vmem,) * 4,
+        name="hand_out",
+    )(*results)
+    return (
+        grad,
+        jnp.transpose(first, (4, 0, 1, 2, 3)),
+        bias[0],
+        jnp.transpose(second, (0, 4, 1, 2, 3)),
+    )
 
 
 def solution(mesh):

time: 102 us -> 76.2 us (0.75)
  local copies, waits for them, and re-layouts: 13.2 us -> 0 us
  Pallas kernels: 87.3 us -> 75.4 us
    pallas_call x1 -> x2, Pallas kernels: 87.3 us -> 75.4 us  [the longest x1 73.9 us: local(): pl.pallas_call(kernel, out_shape=(shapes[0], jax.ShapeDtypeStruct((32, N)...]
    unnamed x25 -> x0, local copies, waits for them, and re-layouts: 8.2 us -> none
    reshape x7 -> x0, local copies, waits for them, and re-layouts: 3.24 us -> none  [the longest x2 0.94 us: local(): first_kernel.reshape(16, 81)]
where the time goes in v1:
time: 76.2 us; the launch traced here: 76 us
  Pallas kernels  75.4 us (99%)
    pallas_call x1, Pallas kernels, local(): pl.pallas_call(kernel, out_shape=(shapes[0], jax.ShapeDtypeStruct((32, N)...  73.9 us
    pallas_call x1, Pallas kernels, local(): pl.pallas_call(hand_out, out_shape=shapes, in_specs=[in_vmem] * 2, out_sp...  1.54 us

profile of v1, /device:TPU:1, one launch (start us, length us, event | category | flops | bytes accessed | tf_op | source)
XLA Modules:
  0.0 76.0 jit_solution(1356677028927254535)
XLA Ops:
  0.6 73.9 %step_backward.1 = (f32[3,2,16,128]{3,2,1,0:T(8,128)}, f32[32,128]{1,0:T(8,128)}) custom-call(f32[4,3,2,16,128]{4,3,2,1,0:T(8,128)} %cot_hbm.1, f32[3,2,16,128]{3,2,1,0:T(8,128)} %vel_hbm.1, f32[8]{0:T(128)} %table_hbm.1, s32[4]{0:T(128)} %index_hbm.1, f32[3,3,3,3,16]{4,3,2,1,0:T(4,128)} %bitcast.6, f32[1,16]{1,0:T(1,128)} %bitcast.8, ...), custom_call_target="tpu_custom_call" | custom-call | tf_op jit(solution)/shard_map/step_backward/pallas_call | solution.py:626
  74.5 1.5 %hand_out.1 = (f32[3,2,16,128]{3,2,1,0:T(8,128)}, f32[3,3,3,3,16]{4,3,2,1,0:T(4,128)}, f32[1,16]{1,0:T(1,128)}, f32[3,3,3,3,16]{4,3,2,1,0:T(4,128)}) custom-call(f32[3,2,16,128]{3,2,1,0:T(8,128)} %get-tuple-element.10.grad, f32[32,128]{1,0:T(8,128)} %get-tuple-element.11.sums), custom_call_target="tpu_custom_call" | custom-call | tf_op jit(solution)/shard_map/hand_out/pallas_call | solution.py:654

commit v2 on v1

--- a/solution.py
+++ b/solution.py
@@ -33,7 +33,12 @@
 def halves(table):
     high = table.astype(np.float32).astype(ml_dtypes.bfloat16)
     low = (table - high.astype(np.float64)).astype(np.float32).astype(ml_dtypes.bfloat16)
-    return np.stack([high, low])
+    return high, low
+
+
+def left_factor(table):
+    high, low = halves(table)
+    return np.stack([high, low, high])
 
 
 def tables():
@@ -57,23 +62,24 @@
             for dx in range(3):
                 for dy in range(3):
                     for dz in range(3):
-                        flat = 4 * (c * 9 + dx * 3 + dy) + dz
+                        tap = c * 27 + dx * 9 + dy * 3 + dz
+                        flat = 4 * (tap // 3) + tap % 3
                         lane = (dy * 3 + dz) * 16 + 4 * (x + dx) + c
                         back = ((2 - dy) * 3 + 2 - dz) * 16 + 4 * (x + 2 - dx) + c
                         spread[0, x, flat, lane] = 1.0
                         spread[1, x, flat, back] = 1.0
-                        gather[0, x, lane, flat] = 1.0
-                        gather[1, x, back, flat] = 1.0
+                        gather[0, x, lane, tap] = 1.0
+                        gather[1, x, back, tap] = 1.0
         spread[0, x, BIAS, 4 * 16 + 3] = 1.0
-        gather[0, x, 4 * 16 + 3, BIAS] = 1.0
+        gather[0, x, 4 * 16 + 3, 81] = 1.0
     exact = ml_dtypes.bfloat16
     return (
-        halves(tz),
-        halves(ex),
-        halves(ty),
-        halves(tyi),
-        halves(txi),
-        halves(zi),
+        left_factor(tz),
+        np.stack([np.concatenate(halves(ex), axis=1), np.pad(halves(ex)[0], ((0, 0), (0, 64)))]),
+        left_factor(ty),
+        left_factor(tyi),
+        left_factor(txi),
+        np.stack([np.concatenate([h, h, l]) for h, l in map(halves, zi)]),
         np.stack([spread[..., :N], spread[..., N:]], axis=2).astype(exact),
         gather.astype(exact),
     )
@@ -90,12 +96,19 @@
     )
 
 
-def dot3(a, b, dims=(1, 0)):
-    return dot(a[0], b[0], dims) + dot(a[0], b[1], dims) + dot(a[1], b[0], dims)
-
-
-def both(ref):
-    return ref[0], ref[1]
+def left(ref):
+    return jnp.concatenate([ref[i] for i in range(ref.shape[0])], axis=1)
+
+
+def right(value, axis=0):
+    high, low = split(value)
+    return jnp.concatenate([high, high, low], axis=axis)
+
+
+def stacked(pair, other, dims):
+    rows = pair[0].shape[0]
+    both = dot(jnp.concatenate(pair, axis=0), other[0], dims)
+    return both[:rows] + both[rows:] + dot(pair[0], other[1], dims)
 
 
 def roll(value, shift):
@@ -122,8 +135,8 @@
 
 
 def x_transform(received, ex):
-    pair = jnp.concatenate(received, axis=1)
-    big = dot3(ex, split(pair))
+    high, low = split(jnp.concatenate(received, axis=1))
+    big = dot(ex, jnp.concatenate([high, high, low, jnp.zeros_like(low)], axis=0), (1, 0))
     lane = lanes()
     first = big[:N, :N] + roll(big[N:, :N], -48)
     second = roll(big[:N, N:], 48) + big[N:, N:]
@@ -208,14 +221,14 @@
     cot_hbm, vel_hbm, table_hbm, index_hbm, first_hbm, bias_hbm, second_hbm, *refs
 ):
     tables_hbm, refs = refs[:TABLES], refs[TABLES:]
-    (out, sums), refs = refs[:2], refs[2:]
+    (out_hbm, sums_hbm), refs = refs[:2], refs[2:]
     (cot, table, index, first, bias, second), refs = refs[:6], refs[6:]
     (tz, ex, ty, tyi, txi, zi, spread, gather), refs = refs[:TABLES], refs[TABLES:]
     (
     send1, recv1, send2, recv2, send3, recv3, send4, recv4,
-    part, recv5, mine, recv6, whole, recv7,
+    part, recv5, mine, recv6, whole, out,
     vext, adv, proj, proj_own, adv_hi, adv_lo, proj_hi, proj_lo,
-    hidden, scattered, gpart, gnat, face_x, face_y, corner, gext,
+    hidden, hid_hi, hid_lo, scattered, gpart, gnat, face_x, face_y, corner, gext,
     flat, own_sem, send_sem, recv_sem, vel_send, vel_recv, e1_send, e1_recv, e2_send, e2_recv,
     load_sem,
     ) = refs
@@ -223,12 +236,37 @@
     n = lax.axis_index("narrow")
     wy, wz, wx = w // 16, w // 4 % 4, w % 4
     zl, core = n // 2, n % 2
-    right, left = lax.rem(w + 1, WIDE), lax.rem(w + WIDE - 1, WIDE)
+    ahead_w, behind_w = lax.rem(w + 1, WIDE), lax.rem(w + WIDE - 1, WIDE)
     above, below = lax.rem(n + 1, NARROW), lax.rem(n + NARROW - 1, NARROW)
 
+    far = lax.rem(n + 4, NARROW)
+    longer = jnp.where(zl < 2, 1, 3)
+
+    def each_wide(act):
+        def offset(i):
+            return jnp.where(i < 2, 2 + i, 3 - i)
+
+        for pair in ((2, longer), (0, lax.rem(longer + 2, 4))):
+            zs = [lax.rem(wz + oz, 4) * 4 for oz in pair]
+
+            def body(i, carry, zs=zs):
+                place = lax.rem(wy + offset(i // 4), 4) * 16 + lax.rem(wx + offset(i % 4), 4)
+                for z in zs:
+                    act(place + z)
+                return carry
+
+            lax.fori_loop(0, 16, body, 0)
+
+    def each_narrow(act):
+        for i in (4, 5, 3, 2, 6, 7, 1):
+            act(lax.rem(far + i, NARROW))
+
+    member = 2 * wx + core
     column = 16 * wy + 4 * wz + zl
-    member = 2 * wx + core
-    stays = wx == zl
+
+    def each_member(act):
+        for i in (4, 5, 3, 2, 6, 7, 1):
+            act(lax.rem(member + i, NARROW))
 
     def each_column(act):
         def body(i, carry):
@@ -239,33 +277,21 @@
 
         lax.fori_loop(0, WIDE - 1, body, 0)
 
-    def each_wide(act):
-        for oz in (2, 1, 3, 0):
-
-            def body(i, carry, oz=oz):
-                y, x = lax.rem(wy + 3 - i // 4, 4), lax.rem(wx + 3 - i % 4, 4)
-                act(y * 16 + lax.rem(wz + oz, 4) * 4 + x)
-                return carry
-
-            lax.fori_loop(0, 15 if oz == 0 else 16, body, 0)
-
-    def each_member(act):
-        for i in (4, 5, 3, 2, 6, 7, 1):
-            act(lax.rem(member + i, NARROW))
-
-    def at_column(p, x):
-        return (p // 16 * 16 + p % 16 // 4 * 4 + x, p % 4 * 2 + core)
-
-    outward = (WIDE, each_column, lambda p: at_column(p, zl), column, w, stays)
-    inward = (WIDE, each_wide, lambda p: (p, member), w, column, stays)
-    columns = (WIDE, each_column, lambda p: at_column(p, wx), column, column, None)
+    across = (WIDE, each_wide, lambda p: (p, far), None, w)
+    narrow = (NARROW, each_narrow, lambda p: (w, lax.rem(p + 4, NARROW)), far, far)
     members = (
         NARROW,
         each_member,
         lambda p: (w - wx + p // 2, n - core + p % 2),
         member,
         member,
-        None,
+    )
+    columns = (
+        WIDE,
+        each_column,
+        lambda p: (p // 16 * 16 + p % 16 // 4 * 4 + wx, p % 4 * 2 + core),
+        column,
+        column,
     )
 
     barrier = pltpu.get_barrier_semaphore()
@@ -273,18 +299,14 @@
     def greet(device):
         pl.semaphore_signal(barrier, inc=1, device_id=device, device_id_type=MESH)
 
-    each_wide(lambda p: greet((p, member)))
-
-    @pl.when(jnp.logical_not(stays))
-    def _():
-        greet((w, member))
-
-    each_member(lambda p: greet(members[2](p)))
+    each_wide(lambda p: greet((p, far)))
     neighbours = (
-        (right, n), (left, n), (w, above), (w, below),
-        (right, above), (right, below), (left, above), (left, below),
-    )
-    for device in neighbours:
+        (ahead_w, n), (behind_w, n), (w, above), (w, below),
+        (ahead_w, above), (ahead_w, below), (behind_w, above), (behind_w, below),
+    )
+    for i in (5, 3, 2, 6, 7, 1):
+        greet((w, lax.rem(n + i, NARROW)))
+    for device in neighbours[:2] + neighbours[4:]:
         greet(device)
 
     loads = [
@@ -318,10 +340,69 @@
             pieces.append(total)
     pieces.append(jnp.zeros((32, N), F32))
     combined = jnp.concatenate(pieces, axis=0)
-    send1[...] = dot3(both(tz), split(combined), (1, 1))
+    send1[...] = dot(left(tz), right(combined, 1), (1, 1))
 
     for load in loads[4:]:
         load.wait()
+
+    pl.semaphore_wait(barrier, WIDE + 12)
+    pending = []
+
+    def copies(moves, sends, recvs):
+        made = []
+        for i, (source, target, device) in enumerate(moves):
+            made.append(
+                pltpu.make_async_remote_copy(
+                    source, target, sends.at[i], recvs.at[i], device_id=device, device_id_type=MESH
+                )
+            )
+        for copy in made:
+            copy.start()
+            pending.append(copy.wait_send)
+        return made
+
+    def exchange(i, group, rows, source, target):
+        size, each, device, own, slot = group
+
+        def block(ref, p):
+            return ref.at[pl.ds(p * rows, rows)]
+
+        def piece(p):
+            return source if source.shape[0] == rows else block(source, p)
+
+        def copy(a, b, to):
+            return pltpu.make_async_remote_copy(
+                a, b, send_sem.at[i], recv_sem.at[i], device_id=to, device_id_type=MESH
+            )
+
+        each(lambda p: copy(piece(p), block(target, slot), device(p)).start())
+        some = target if own is None else target.at[pl.ds(0, (size - 1) * rows)]
+        others = copy(some, some, (w, far))
+        pending.append(others.wait_send)
+        if own is None:
+            return others.wait_recv
+        keep = pltpu.make_async_copy(piece(own), block(target, slot), own_sem.at[i])
+        keep.start()
+
+        def arrived():
+            keep.wait()
+            others.wait_recv()
+
+        return arrived
+
+    got1 = exchange(0, across, 2, send1, recv1)
+
+    low, high, full = pl.ds(8, 2), pl.ds(22, 2), pl.ds(8, 16)
+    moves = []
+    for device, rows, xs, ys in zip(
+        neighbours,
+        (full, full, high, low, high, low, high, low),
+        (0, 4, 2, 2, 0, 0, 4, 4),
+        (full, full, pl.ds(6, 2), pl.ds(24, 2)) + (pl.ds(6, 2), pl.ds(24, 2)) * 2,
+    ):
+        source = vext.at[:, pl.ds(2, 2), rows, :]
+        moves.append((source, vext.at[:, pl.ds(xs, 2), ys, :], device))
+    vel_copies = copies(moves, vel_send, vel_recv)
 
     taps_first, taps_second = [], []
     for kind, (ref, place) in enumerate(((first, taps_first), (second, taps_second))):
@@ -343,98 +424,20 @@
     sublane = lax.broadcasted_iota(jnp.int32, (288, N), 0) % 16
     adv[...] = jnp.where(sublane == 3, 1.0, 0.0)
 
-    pl.semaphore_wait(barrier, WIDE + NARROW + 6 + jnp.where(stays, 0, 1))
-    pending = []
-
-    def copies(moves, sends, recvs):
-        made = []
-        for i, (source, target, device) in enumerate(moves):
-            made.append(
-                pltpu.make_async_remote_copy(
-                    source, target, sends.at[i], recvs.at[i], device_id=device, device_id_type=MESH
-                )
-            )
-        for copy in made:
-            copy.start()
-            pending.append(copy.wait_send)
-        return made
-
-    def exchange(i, group, rows, source, target):
-        size, each, device, own, slot, kept = group
-
-        def block(ref, p):
-            return ref.at[pl.ds(p * rows, rows)]
-
-        def piece(p):
-            return source if source.shape[0] == rows else block(source, p)
-
-        def copy(a, b, to):
-            return pltpu.make_async_remote_copy(
-                a, b, send_sem.at[i], recv_sem.at[i], device_id=to, device_id_type=MESH
-            )
-
-        def act(p):
-            copy(piece(p), block(target, slot), device(p)).start()
-
-        each(act)
-        keep = pltpu.make_async_copy(piece(own), block(target, slot), own_sem.at[i])
-        some = target.at[pl.ds(0, (size - 1) * rows)]
-        others = copy(some, some, (right, n))
-        if kept is None:
-            keep.start()
-            pending.append(others.wait_send)
-
-            def arrived():
-                keep.wait()
-                others.wait_recv()
-
-            return arrived
-        everyone = copy(target, target, (right, n))
-
-        def either(here, there):
-            pl.when(kept)(here)
-            pl.when(jnp.logical_not(kept))(there)
-
-        either(lambda: keep.start(), lambda: act(own))
-        pending.append(lambda: either(lambda: others.wait_send(), lambda: everyone.wait_send()))
-
-        def arrived():
-            def here():
-                keep.wait()
-                others.wait_recv()
-
-            either(here, lambda: everyone.wait_recv())
-
-        return arrived
-
-    got1 = exchange(0, outward, 2, send1, recv1)
-
     got1()
     kz_rows = [recv1[pl.ds(k, 64, stride=2), :] for k in range(2)]
-    send2[...] = x_transform(kz_rows, both(ex))
-    got2 = exchange(1, members, 16, send2, recv2)
-
-    low, high, full = pl.ds(8, 2), pl.ds(22, 2), pl.ds(8, 16)
-    moves = []
-    for device, rows, xs, ys in zip(
-        neighbours,
-        (full, full, high, low, high, low, high, low),
-        (0, 4, 2, 2, 0, 0, 4, 4),
-        (full, full, pl.ds(6, 2), pl.ds(24, 2)) + (pl.ds(6, 2), pl.ds(24, 2)) * 2,
-    ):
-        source = vext.at[:, pl.ds(2, 2), rows, :]
-        moves.append((source, vext.at[:, pl.ds(xs, 2), ys, :], device))
-    vel_copies = copies(moves, vel_send, vel_recv)
+    send2[...] = x_transform(kz_rows, left(ex))
+    got2 = exchange(1, narrow, 16, send2, recv2)
 
     got2()
-    spectrum = dot3(both(ty), split(swap_blocks(recv2[...])))
-    spectrum = project(spectrum, column, member)
-    send3[...] = dot3(both(tyi), split(spectrum))
-    got3 = exchange(2, members, 24, send3, recv3)
+    spectrum = dot(left(ty), right(swap_blocks(recv2[...])), (1, 0))
+    spectrum = project(spectrum, w, far)
+    send3[...] = dot(left(tyi), right(spectrum), (1, 0))
+    got3 = exchange(2, narrow, 24, send3, recv3)
 
     got3()
-    send4[...] = dot3(both(txi), split(pack_rows(recv3[...])))
-    got4 = exchange(3, inward, 4, send4, recv4)
+    send4[...] = dot(left(txi), right(pack_rows(recv3[...])), (1, 0))
+    got4 = exchange(3, across, 4, send4, recv4)
 
     for copy in vel_copies:
         copy.wait_recv()
@@ -459,12 +462,15 @@
             adv[272 + at : 273 + at] = done[24:25]
     taps(adv[...], adv_hi, adv_lo)
     adv_taps = (adv_hi[...], adv_lo[...])
-    hidden[...] = jnp.tanh(dot3(taps_first, adv_taps))
+    hid = jnp.tanh(stacked(taps_first, adv_taps, (1, 0)))
+    hidden[...] = 1.0 - hid * hid
+    hid_hi[...], hid_lo[...] = split(hid)
 
     got4()
+    high, low = split(jnp.concatenate([recv4[pl.ds(x, 64, stride=4), :] for x in range(4)], axis=1))
+    fields = dot(jnp.concatenate([high, low, high], axis=0), left(zi), (0, 0))
     for x in range(4):
-        rows = split(recv4[pl.ds(x, 64, stride=4), :])
-        even, odd = (dot3(rows, (zi[0, k], zi[1, k]), (0, 0)) for k in range(2))
+        even, odd = fields[N * x : N * x + N, :N], fields[N * x : N * x + N, N:]
         inner = even[:48] + odd[48:96]
         outer = even[96:104] + odd[104:112]
         for c in range(3):
@@ -477,10 +483,29 @@
 
     taps(proj[...], proj_hi, proj_lo)
     proj_taps = (proj_hi[...], proj_lo[...])
-    hid = hidden[...]
-    pre = split(dot3(taps_second, proj_taps) * (1.0 - hid * hid))
-
-    scattered[...] = dot3(taps_first, pre, (0, 0))
+    pre = split(stacked(taps_second, proj_taps, (1, 0)) * hidden[...])
+
+    gradients = []
+    for kind, (rows, cols) in enumerate(((pre, adv_taps), ((hid_hi[...], hid_lo[...]), proj_taps))):
+        raw = stacked(rows, cols, (1, 1))
+        total = jnp.zeros((16, N), F32)
+        for x in range(2):
+            for piece in split(raw[16 * x : 16 * x + 16]):
+                total = total + dot(piece, gather[kind, x], (1, 0))
+        gradients.append(total)
+    lane = lanes()
+    beside = jnp.logical_and(lane >= 82, lane < 123)
+    spare = gradients[1][8:]
+    part[0:8] = jnp.where(beside, roll(spare, 82), gradients[0][:8])
+    part[8:16] = jnp.where(beside, roll(spare, 41), gradients[0][8:])
+    part[16:24] = gradients[1][:8]
+    got5 = exchange(4, members, 3, part, recv5)
+
+    scattered[...] = dot(
+        jnp.concatenate([*taps_first, taps_first[0]], axis=0),
+        jnp.concatenate([pre[0], pre[0], pre[1]], axis=0),
+        (0, 0),
+    )
     for y in range(18):
         moved = []
         for dz in range(3):
@@ -502,36 +527,30 @@
     row_0, row_7, row_8, row_23, row_24 = (pl.ds(r, 1) for r in (0, 7, 8, 23, 24))
     e1 = copies(
         [
-            (gnat.at[:, 3, own_y, :], face_x.at[0], (right, n)),
-            (gnat.at[:, 0, own_y, :], face_x.at[1], (left, n)),
+            (gnat.at[:, 3, own_y, :], face_x.at[0], (ahead_w, n)),
+            (gnat.at[:, 0, own_y, :], face_x.at[1], (behind_w, n)),
             (gnat.at[:, own_x, row_24, :], face_y.at[0, :, :, row_0, :], (w, above)),
             (gnat.at[:, own_x, row_7, :], face_y.at[1, :, :, row_7, :], (w, below)),
-            (gnat.at[:, 3, row_24, :], corner.at[0, :, row_0, :], (right, above)),
-            (gnat.at[:, 3, row_7, :], corner.at[1, :, row_7, :], (right, below)),
-            (gnat.at[:, 0, row_24, :], corner.at[2, :, row_0, :], (left, above)),
-            (gnat.at[:, 0, row_7, :], corner.at[3, :, row_7, :], (left, below)),
+            (gnat.at[:, 3, row_24, :], corner.at[0, :, row_0, :], (ahead_w, above)),
+            (gnat.at[:, 3, row_7, :], corner.at[1, :, row_7, :], (ahead_w, below)),
+            (gnat.at[:, 0, row_24, :], corner.at[2, :, row_0, :], (behind_w, above)),
+            (gnat.at[:, 0, row_7, :], corner.at[3, :, row_7, :], (behind_w, below)),
         ],
         e1_send,
         e1_recv,
     )
 
-    for kind, (rows, cols) in enumerate(((pre, adv_taps), (split(hid), proj_taps))):
-        raw = dot3(rows, cols, (1, 1))
-        total = jnp.zeros((16, N), F32)
-        for x in range(2):
-            for piece in split(raw[16 * x : 16 * x + 16]):
-                total = total + dot(piece, gather[kind, x], (1, 0))
-        part[16 * kind : 16 * kind + 16] = total
-    got5 = exchange(4, members, 4, part, recv5)
-
     got5()
 
-    def fold(value):
-        value = jnp.sum(value.reshape(value.shape[0] // 8, 8, N), axis=0)
-        return value[0:4] + value[4:8]
-
-    mine[...] = fold(recv5[...])
-    got6 = exchange(5, columns, 4, mine, recv6)
+    def fold(ref):
+        count = ref.shape[0] // 3
+        return [
+            jnp.sum(ref[pl.ds(row, count, stride=3), :], axis=0, keepdims=True) for row in range(3)
+        ]
+
+    for row, total in enumerate(fold(recv5)):
+        mine[row : row + 1] = total
+    got6 = exchange(5, columns, 3, mine, recv6)
 
     for copy in e1:
         copy.wait_recv()
@@ -544,8 +563,8 @@
             gext[c, x + 1, 16:24] = end
     e2 = copies(
         [
-            (gext.at[:, 1, own_y, :], gext.at[:, 3, own_y, :], (left, n)),
-            (gext.at[:, 2, own_y, :], gext.at[:, 0, own_y, :], (right, n)),
+            (gext.at[:, 1, own_y, :], gext.at[:, 3, own_y, :], (behind_w, n)),
+            (gext.at[:, 2, own_y, :], gext.at[:, 0, own_y, :], (ahead_w, n)),
             (gext.at[:, own_x, row_8, :], gext.at[:, own_x, row_24, :], (w, below)),
             (gext.at[:, own_x, row_23, :], gext.at[:, own_x, row_7, :], (w, above)),
         ],
@@ -553,8 +572,9 @@
         e2_recv,
     )
     got6()
-    whole[...] = fold(recv6[...]) * (N * N * N) ** -0.5
-    got7 = exchange(6, members, 4, whole, recv7)
+    for row, total in enumerate(fold(recv6)):
+        whole[row : row + 1] = total * (N * N * N) ** -0.5
+    got7 = exchange(6, members, 3, whole, sums_hbm)
 
     for copy in e2:
         copy.wait_recv()
@@ -593,21 +613,25 @@
         for c in range(3):
             out[c, x] = (g[c] - STEP * totals[c] - STEP * slopes[c])[8:24]
 
+    store = pltpu.make_async_copy(out, out_hbm, load_sem.at[7 + TABLES])
+    store.start()
     got7()
-    sums[...] = recv7[...]
-
+    store.wait()
     for wait in pending:
         wait()
 
 
 def hand_out(grad, sums, out, out_first, out_bias, out_second):
     out[...] = grad[...]
+    lane = lanes()
+    spare = jnp.where(lane < 41, roll(sums[0:8], -82), roll(sums[8:16], -41))
+    both = (sums[0:16], jnp.concatenate([sums[16:24], spare], axis=0))
     for kind, ref in enumerate((out_first, out_second)):
-        turned = sums[16 * kind : 16 * kind + 16].T
+        turned = both[kind].T
         for tap in range(27):
-            ref[tap // 9, tap // 3 % 3, tap % 3] = turned[4 * tap : 4 * tap + 3]
+            ref[tap // 9, tap // 3 % 3, tap % 3] = turned[3 * tap : 3 * tap + 3]
         if kind == 0:
-            out_bias[...] = turned[BIAS : BIAS + 1]
+            out_bias[...] = turned[81:82]
 
 
 def local(velocity, cotangents, lead_table, lead_index, first_kernel, first_bias, second_kernel):
@@ -625,22 +649,23 @@
     )
     results = pl.pallas_call(
         kernel,
-        out_shape=(shapes[0], jax.ShapeDtypeStruct((32, N), F32)),
+        out_shape=(shapes[0], jax.ShapeDtypeStruct((24, N), F32)),
         in_specs=[anywhere] * (7 + TABLES),
-        out_specs=(in_vmem,) * 2,
+        out_specs=(anywhere,) * 2,
         scratch_shapes=[
             v(4, 3, 2, 16, N), pltpu.SMEM((8,), F32), pltpu.SMEM((4,), jnp.int32),
             v(3, 3, 3, 3, 16), v(1, 16), v(3, 3, 3, 3, 16),
             *[v(*t.shape, kind=BF16) for t in constants],
             v(128, N), v(128, N), v(128, N), v(128, N), v(192, N), v(192, N), v(256, N), v(256, N),
-            v(32, N), v(32, N), v(4, N), v(256, N), v(4, N), v(32, N),
+            v(24, N), v(24, N), v(3, N), v(192, N), v(3, N), v(3, 2, 16, N),
             v(3, 6, 32, N), v(288, N), v(288, N), v(3, 2, 16, N),
             v(144, 2048, kind=BF16), v(144, 2048, kind=BF16),
             v(144, 2048, kind=BF16), v(144, 2048, kind=BF16),
-            v(32, 2048), v(144, 2048), v(288, N), v(3, 4, 32, N),
+            v(32, 2048), v(32, 2048, kind=BF16), v(32, 2048, kind=BF16),
+            v(144, 2048), v(288, N), v(3, 4, 32, N),
             v(2, 3, 16, N), v(2, 3, 2, 8, N), v(4, 3, 8, N), v(3, 4, 32, N),
             v(N, N), dma((7,)), dma((7,)), dma((7,)), dma((8,)), dma((8,)), dma((8,)), dma((8,)),
-            dma((4,)), dma((4,)), dma((7 + TABLES,)),
+            dma((4,)), dma((4,)), dma((8 + TABLES,)),
         ],
         compiler_params=pltpu.CompilerParams(
             collective_id=0, has_side_effects=True, vmem_limit_bytes=60 * 1024 * 1024

time: 76.2 us -> 70.8 us (0.929)
  Pallas kernels: 75.4 us -> 69.9 us
    pallas_call x1, Pallas kernels: 73.9 us -> 68.4 us  [local(): pl.pallas_call(kernel, out_shape=(shapes[0], jax.ShapeDtypeStruct((24, N)...]
where the time goes in v2:
time: 70.8 us; the launch traced here: 70.6 us
  Pallas kernels  69.9 us (99%)
    pallas_call x1, Pallas kernels, local(): pl.pallas_call(kernel, out_shape=(shapes[0], jax.ShapeDtypeStruct((24, N)...  68.4 us
    pallas_call x1, Pallas kernels, local(): pl.pallas_call(hand_out, out_shape=shapes, in_specs=[in_vmem] * 2, out_sp...  1.58 us

profile of v2, /device:TPU:1, one launch (start us, length us, event | category | flops | bytes accessed | tf_op | source)
XLA Modules:
  0.0 70.6 jit_solution(1199762450570749984)
XLA Ops:
  0.6 68.4 %step_backward.1 = (f32[3,2,16,128]{3,2,1,0:T(8,128)}, f32[24,128]{1,0:T(8,128)}) custom-call(f32[4,3,2,16,128]{4,3,2,1,0:T(8,128)} %cot_hbm.1, f32[3,2,16,128]{3,2,1,0:T(8,128)} %vel_hbm.1, f32[8]{0:T(128)} %table_hbm.1, s32[4]{0:T(128)} %index_hbm.1, f32[3,3,3,3,16]{4,3,2,1,0:T(4,128)} %bitcast.6, f32[1,16]{1,0:T(1,128)} %bitcast.8, ...), custom_call_target="tpu_custom_call" | custom-call | tf_op jit(solution)/shard_map/step_backward/pallas_call | solution.py:650
  69.0 1.6 %hand_out.1 = (f32[3,2,16,128]{3,2,1,0:T(8,128)}, f32[3,3,3,3,16]{4,3,2,1,0:T(4,128)}, f32[1,16]{1,0:T(1,128)}, f32[3,3,3,3,16]{4,3,2,1,0:T(4,128)}) custom-call(f32[3,2,16,128]{3,2,1,0:T(8,128)} %get-tuple-element.10.grad, f32[24,128]{1,0:T(8,128)} %get-tuple-element.11.sums), custom_call_target="tpu_custom_call" | custom-call | tf_op jit(solution)/shard_map/hand_out/pallas_call | solution.py:679

commit v3 on v2

--- a/solution.py
+++ b/solution.py
@@ -17,7 +17,8 @@
 NARROW = 8
 STEP = 0.25
 BIAS = 108
-TABLES = 8
+TABLES = 7
+ORDER = (2, 0, 1)
 
 
 def basis(kind, wave):
@@ -41,20 +42,21 @@
     return np.stack([high, low, high])
 
 
+def thin_factor(table):
+    high, low = halves(table)
+    return np.stack([np.concatenate([high, low], axis=1), np.pad(high, ((0, 0), (0, 64)))])
+
+
 def tables():
-    tz = np.stack([basis(i % 2, i // 2) for i in range(N)])
-    tx = np.stack([basis((i % 16) // 8, 8 * (i // 16) + i % 8) for i in range(N)])
-    ty = np.stack([basis(i // 64, i % 64) for i in range(N)])
+    tz = np.stack([basis((i % 16) // 8, 8 * (i // 16) + i % 8) for i in range(N)])
+    ty = np.stack([basis(i % 2, i // 2) for i in range(N)])
+    tx = np.stack([basis(i // 64, i % 64) for i in range(N)])
     ex = np.concatenate([tx[:, 0::2], tx[:, 1::2]], axis=0)
-    rows = []
+    txi = np.stack([tx[:, (2 * w - 1 + x) % N] for x in range(4) for w in range(WIDE)])
+    cells = []
     for n in range(NARROW):
-        cells = [16 * n + r for r in range(16)] + [16 * n - 1, 16 * n + 16]
-        for y in cells:
-            rows.append(ty[:, y % N])
-        rows.extend([np.zeros(N)] * 6)
-    tyi = np.stack(rows)
-    txi = np.stack([tx[:, (2 * w - 1 + x) % N] for w in range(WIDE) for x in range(4)])
-    zi = np.stack([tz[0::2], tz[1::2]])
+        cells += [16 * n + r for r in range(16)] + [16 * n - 1, 16 * n + 16] + [0] * 6
+    tyi = np.concatenate([ty[k::2, np.array(cells) % N].T for k in range(2)], axis=0)
     spread = np.zeros((2, 2, N, 256))
     gather = np.zeros((2, 2, 144, N))
     for x in range(2):
@@ -75,11 +77,10 @@
     exact = ml_dtypes.bfloat16
     return (
         left_factor(tz),
-        np.stack([np.concatenate(halves(ex), axis=1), np.pad(halves(ex)[0], ((0, 0), (0, 64)))]),
         left_factor(ty),
-        left_factor(tyi),
+        thin_factor(ex),
         left_factor(txi),
-        np.stack([np.concatenate([h, h, l]) for h, l in map(halves, zi)]),
+        thin_factor(tyi),
         np.stack([spread[..., :N], spread[..., N:]], axis=2).astype(exact),
         gather.astype(exact),
     )
@@ -120,7 +121,6 @@
 
 
 def swap_blocks(m):
-    m = m.T
     lane = lanes()
     for bit in (1, 2, 4):
         size = 16 * bit
@@ -134,13 +134,16 @@
     return m
 
 
-def x_transform(received, ex):
-    high, low = split(jnp.concatenate(received, axis=1))
-    big = dot(ex, jnp.concatenate([high, high, low, jnp.zeros_like(low)], axis=0), (1, 0))
+def thin(table, value):
+    high, low = split(value)
+    return dot(table, jnp.concatenate([high, high, low, jnp.zeros_like(low)], axis=0), (1, 0))
+
+
+def from_pairs(even, odd, first, second):
     lane = lanes()
-    first = big[:N, :N] + roll(big[N:, :N], -48)
-    second = roll(big[:N, N:], 48) + big[N:, N:]
-    return jnp.where(lane < 48, first, jnp.where(lane < 96, second, 0.0))
+    one = even[:, first] + roll(odd[:, first], -48)
+    two = roll(even[:, second], 48) + odd[:, second]
+    return jnp.where(lane < 48, one, jnp.where(lane < 96, two, 0.0))
 
 
 def project(field, w, n):
@@ -185,22 +188,13 @@
     return field + derive(main) - nyquist * rest
 
 
-def pack_rows(received):
-    lane = lanes()
-    inner = jnp.concatenate([received[24 * i : 24 * i + 16] for i in range(NARROW)], axis=0)
+def z_blocks(received, tile):
+    rows = [48 * n + 24 * tile for n in range(NARROW)]
+    inner = swap_blocks(jnp.concatenate([received[r : r + 16] for r in rows], axis=0))
     none = jnp.zeros((8, N), F32)
-    outer = []
-    for i in range(NARROW):
-        outer.extend([received[24 * i + 16 : 24 * i + 24], none])
-    inner = swap_blocks(inner)
+    outer = [piece for r in rows for piece in (received[r + 16 : r + 24], none)]
     outer = swap_blocks(jnp.concatenate(outer, axis=0))
-    full = jnp.where(lane < 96, inner, 0.0)
-    for k in range(2):
-        for c in range(3):
-            place = 96 + 8 * k + 2 * c
-            here = jnp.logical_and(lane >= place, lane < place + 2)
-            full = jnp.where(here, roll(outer, place - 16 * (3 * k + c)), full)
-    return full
+    return inner[:96], [outer[16 * b : 16 * b + 8] for b in range(6)]
 
 
 def taps(field, high_ref, low_ref):
@@ -223,14 +217,14 @@
     tables_hbm, refs = refs[:TABLES], refs[TABLES:]
     (out_hbm, sums_hbm), refs = refs[:2], refs[2:]
     (cot, table, index, first, bias, second), refs = refs[:6], refs[6:]
-    (tz, ex, ty, tyi, txi, zi, spread, gather), refs = refs[:TABLES], refs[TABLES:]
+    (tz, ty, ex, txi, tyi, spread, gather), refs = refs[:TABLES], refs[TABLES:]
     (
     send1, recv1, send2, recv2, send3, recv3, send4, recv4,
     part, recv5, mine, recv6, whole, out,
     vext, adv, proj, proj_own, adv_hi, adv_lo, proj_hi, proj_lo,
     hidden, hid_hi, hid_lo, scattered, gpart, gnat, face_x, face_y, corner, gext,
     flat, own_sem, send_sem, recv_sem, vel_send, vel_recv, e1_send, e1_recv, e2_send, e2_recv,
-    load_sem,
+    load_sem, token,
     ) = refs
     w = lax.axis_index("wide")
     n = lax.axis_index("narrow")
@@ -257,9 +251,16 @@
 
             lax.fori_loop(0, 16, body, 0)
 
+    def each_plane(act):
+        def body(i, carry):
+            act(lax.rem(wy + i // 4, 4) * 16 + wz * 4 + lax.rem(wx + i % 4, 4))
+            return carry
+
+        lax.fori_loop(1, 16, body, 0)
+
     def each_narrow(act):
         for i in (4, 5, 3, 2, 6, 7, 1):
-            act(lax.rem(far + i, NARROW))
+            act(lax.rem(n + i, NARROW))
 
     member = 2 * wx + core
     column = 16 * wy + 4 * wz + zl
@@ -278,7 +279,7 @@
         lax.fori_loop(0, WIDE - 1, body, 0)
 
     across = (WIDE, each_wide, lambda p: (p, far), None, w)
-    narrow = (NARROW, each_narrow, lambda p: (w, lax.rem(p + 4, NARROW)), far, far)
+    narrow = (NARROW, each_narrow, lambda p: (w, p), n, n)
     members = (
         NARROW,
         each_member,
@@ -299,13 +300,14 @@
     def greet(device):
         pl.semaphore_signal(barrier, inc=1, device_id=device, device_id_type=MESH)
 
-    each_wide(lambda p: greet((p, far)))
+    for i in (2, 1, 3):
+        greet((16 * wy + 4 * lax.rem(wz + i, 4) + wx, far))
+    each_plane(lambda p: greet((p, n)))
     neighbours = (
         (ahead_w, n), (behind_w, n), (w, above), (w, below),
         (ahead_w, above), (ahead_w, below), (behind_w, above), (behind_w, below),
     )
-    for i in (5, 3, 2, 6, 7, 1):
-        greet((w, lax.rem(n + i, NARROW)))
+    each_narrow(lambda p: greet((w, p)))
     for device in neighbours[:2] + neighbours[4:]:
         greet(device)
 
@@ -322,7 +324,7 @@
                 (bias_hbm, bias),
                 (second_hbm, second),
             ]
-            + list(zip(tables_hbm[1:], (ex, ty, tyi, txi, zi, spread, gather)))
+            + list(zip(tables_hbm[1:], (ty, ex, txi, tyi, spread, gather)))
         )
     ]
     for load in loads:
@@ -333,7 +335,7 @@
     weight = [table[index[l]] for l in range(4)]
     pieces = []
     for x in range(2):
-        for c in range(3):
+        for c in ORDER:
             total = weight[0] * cot[0, c, x]
             for l in range(1, 4):
                 total = total + weight[l] * cot[l, c, x]
@@ -345,7 +347,7 @@
     for load in loads[4:]:
         load.wait()
 
-    pl.semaphore_wait(barrier, WIDE + 12)
+    pl.semaphore_wait(barrier, 3 + 15 + 7 + 6)
     pending = []
 
     def copies(moves, sends, recvs):
@@ -361,11 +363,11 @@
             pending.append(copy.wait_send)
         return made
 
-    def exchange(i, group, rows, source, target):
+    def exchange(i, group, rows, source, target, used=None):
         size, each, device, own, slot = group
 
         def block(ref, p):
-            return ref.at[pl.ds(p * rows, rows)]
+            return ref.at[pl.ds(p * rows, used or rows)]
 
         def piece(p):
             return source if source.shape[0] == rows else block(source, p)
@@ -376,7 +378,7 @@
             )
 
         each(lambda p: copy(piece(p), block(target, slot), device(p)).start())
-        some = target if own is None else target.at[pl.ds(0, (size - 1) * rows)]
+        some = target if own is None else target.at[pl.ds(0, (size - 1) * (used or rows))]
         others = copy(some, some, (w, far))
         pending.append(others.wait_send)
         if own is None:
@@ -390,7 +392,17 @@
 
         return arrived
 
-    got1 = exchange(0, across, 2, send1, recv1)
+    got1 = exchange(0, narrow, 16, send1, recv1)
+
+    def tell(p):
+        pl.semaphore_signal(token, inc=1, device_id=(p, n), device_id_type=MESH)
+
+    each_plane(tell)
+
+    got1()
+    send2[...] = dot(left(ty), right(swap_blocks(recv1[...].T)), (1, 0))
+    pl.semaphore_wait(token, 15)
+    got2 = exchange(1, across, 2, send2, recv2)
 
     low, high, full = pl.ds(8, 2), pl.ds(22, 2), pl.ds(8, 16)
     moves = []
@@ -424,20 +436,18 @@
     sublane = lax.broadcasted_iota(jnp.int32, (288, N), 0) % 16
     adv[...] = jnp.where(sublane == 3, 1.0, 0.0)
 
-    got1()
-    kz_rows = [recv1[pl.ds(k, 64, stride=2), :] for k in range(2)]
-    send2[...] = x_transform(kz_rows, left(ex))
-    got2 = exchange(1, narrow, 16, send2, recv2)
-
     got2()
-    spectrum = dot(left(ty), right(swap_blocks(recv2[...])), (1, 0))
-    spectrum = project(spectrum, w, far)
-    send3[...] = dot(left(tyi), right(spectrum), (1, 0))
-    got3 = exchange(2, narrow, 24, send3, recv3)
-
-    got3()
-    send4[...] = dot(left(txi), right(pack_rows(recv3[...])), (1, 0))
-    got4 = exchange(3, across, 4, send4, recv4)
+    pair = jnp.concatenate([recv2[pl.ds(k, 64, stride=2), :] for k in range(2)], axis=1)
+    field = thin(left(ex), pair)
+    first_half, second_half = slice(0, N), slice(N, 2 * N)
+    spectrum = project(from_pairs(field[:N], field[N:], first_half, second_half), w, far)
+    fields = dot(left(txi), right(spectrum), (1, 0))
+    lane = lanes()
+    last = fields[192:256]
+    for x in range(3):
+        rows = jnp.where(lane < 96, fields[64 * x : 64 * x + 64], roll(last, 96 - 32 * x))
+        send3[pl.ds(x, 64, stride=3), :] = rows
+    got3 = exchange(2, across, 3, send3, recv3)
 
     for copy in vel_copies:
         copy.wait_recv()
@@ -466,20 +476,38 @@
     hidden[...] = 1.0 - hid * hid
     hid_hi[...], hid_lo[...] = split(hid)
 
+    got3()
+    rows = [recv3[pl.ds(x, 64, stride=3), :] for x in range(3)]
+    rows.append(
+        jnp.where(lane < 32, roll(rows[0], 32), jnp.where(lane < 64, roll(rows[1], 64), roll(rows[2], 96)))
+    )
+    field = thin(left(tyi), jnp.concatenate(rows, axis=1))
+    for tile in range(2):
+        columns_of = [slice(N * x, N * x + N) for x in (2 * tile, 2 * tile + 1)]
+        pieces = from_pairs(field[:192], field[192:], *columns_of)
+        for i in range(NARROW):
+            send4[48 * i + 24 * tile : 48 * i + 24 * tile + 24] = pieces[24 * i : 24 * i + 24]
+    got4 = exchange(3, narrow, 48, send4, recv4, 42)
+
     got4()
-    high, low = split(jnp.concatenate([recv4[pl.ds(x, 64, stride=4), :] for x in range(4)], axis=1))
-    fields = dot(jnp.concatenate([high, low, high], axis=0), left(zi), (0, 0))
+    inner_rows, outer_rows = [], []
+    for tile in range(2):
+        inner, outer = z_blocks(recv4[...], tile)
+        inner_rows.append(inner)
+        outer_rows.extend(outer)
+    spectra = right(jnp.concatenate(inner_rows + outer_rows, axis=0), 1)
+    fields = dot(spectra, jnp.concatenate([tz[i] for i in range(3)], axis=0), (1, 0))
     for x in range(4):
-        even, odd = fields[N * x : N * x + N, :N], fields[N * x : N * x + N, N:]
-        inner = even[:48] + odd[48:96]
-        outer = even[96:104] + odd[104:112]
-        for c in range(3):
+        for place, c in enumerate(ORDER):
+            block = 3 * x + place
+            inner = fields[16 * block : 16 * block + 16]
+            outer = fields[192 + 8 * block : 192 + 8 * block + 8]
             at = 4 * x + c
-            proj[at : at + 1] = outer[2 * c : 2 * c + 1]
-            proj[pl.ds(16 + at, 16, stride=16), :] = inner[16 * c : 16 * c + 16]
-            proj[272 + at : 273 + at] = outer[2 * c + 1 : 2 * c + 2]
+            proj[at : at + 1] = outer[0:1]
+            proj[pl.ds(16 + at, 16, stride=16), :] = inner
+            proj[272 + at : 273 + at] = outer[1:2]
             if x in (1, 2):
-                proj_own[c, x - 1] = inner[16 * c : 16 * c + 16]
+                proj_own[c, x - 1] = inner
 
     taps(proj[...], proj_hi, proj_lo)
     proj_taps = (proj_hi[...], proj_lo[...])
@@ -656,7 +684,7 @@
             v(4, 3, 2, 16, N), pltpu.SMEM((8,), F32), pltpu.SMEM((4,), jnp.int32),
             v(3, 3, 3, 3, 16), v(1, 16), v(3, 3, 3, 3, 16),
             *[v(*t.shape, kind=BF16) for t in constants],
-            v(128, N), v(128, N), v(128, N), v(128, N), v(192, N), v(192, N), v(256, N), v(256, N),
+            v(128, N), v(128, N), v(128, N), v(128, N), v(192, N), v(192, N), v(384, N), v(384, N),
             v(24, N), v(24, N), v(3, N), v(192, N), v(3, N), v(3, 2, 16, N),
             v(3, 6, 32, N), v(288, N), v(288, N), v(3, 2, 16, N),
             v(144, 2048, kind=BF16), v(144, 2048, kind=BF16),
@@ -665,7 +693,7 @@
             v(144, 2048), v(288, N), v(3, 4, 32, N),
             v(2, 3, 16, N), v(2, 3, 2, 8, N), v(4, 3, 8, N), v(3, 4, 32, N),
             v(N, N), dma((7,)), dma((7,)), dma((7,)), dma((8,)), dma((8,)), dma((8,)), dma((8,)),
-            dma((4,)), dma((4,)), dma((8 + TABLES,)),
+            dma((4,)), dma((4,)), dma((8 + TABLES,)), pltpu.SemaphoreType.REGULAR,
         ],
         compiler_params=pltpu.CompilerParams(
             collective_id=0, has_side_effects=True, vmem_limit_bytes=60 * 1024 * 1024

time: 70.8 us -> 67.7 us (0.956)
  Pallas kernels: 69.9 us -> 66.9 us
    pallas_call x1, Pallas kernels: 68.4 us -> 65.3 us  [local(): pl.pallas_call(kernel, out_shape=(shapes[0], jax.ShapeDtypeStruct((24, N)...]
where the time goes in v3:
time: 67.7 us; the launch traced here: 67.5 us
  Pallas kernels  66.9 us (99%)
    pallas_call x1, Pallas kernels, local(): pl.pallas_call(kernel, out_shape=(shapes[0], jax.ShapeDtypeStruct((24, N)...  65.3 us
    pallas_call x1, Pallas kernels, local(): pl.pallas_call(hand_out, out_shape=shapes, in_specs=[in_vmem] * 2, out_sp...  1.58 us

profile of v3, /device:TPU:1, one launch (start us, length us, event | category | flops | bytes accessed | tf_op | source)
XLA Modules:
  0.0 67.5 jit_solution(9078493596409879607)
XLA Ops:
  0.6 65.3 %step_backward.1 = (f32[3,2,16,128]{3,2,1,0:T(8,128)}, f32[24,128]{1,0:T(8,128)}) custom-call(f32[4,3,2,16,128]{4,3,2,1,0:T(8,128)} %cot_hbm.1, f32[3,2,16,128]{3,2,1,0:T(8,128)} %vel_hbm.1, f32[8]{0:T(128)} %table_hbm.1, s32[4]{0:T(128)} %index_hbm.1, f32[3,3,3,3,16]{4,3,2,1,0:T(4,128)} %bitcast.6, f32[1,16]{1,0:T(1,128)} %bitcast.8, ...), custom_call_target="tpu_custom_call" | custom-call | tf_op jit(solution)/shard_map/step_backward/pallas_call | solution.py:678
  65.9 1.6 %hand_out.1 = (f32[3,2,16,128]{3,2,1,0:T(8,128)}, f32[3,3,3,3,16]{4,3,2,1,0:T(4,128)}, f32[1,16]{1,0:T(1,128)}, f32[3,3,3,3,16]{4,3,2,1,0:T(4,128)}) custom-call(f32[3,2,16,128]{3,2,1,0:T(8,128)} %get-tuple-element.10.grad, f32[24,128]{1,0:T(8,128)} %get-tuple-element.11.sums), custom_call_target="tpu_custom_call" | custom-call | tf_op jit(solution)/shard_map/hand_out/pallas_call | solution.py:707

commit v4 on v3

--- a/solution.py
+++ b/solution.py
@@ -188,13 +188,13 @@
     return field + derive(main) - nyquist * rest
 
 
-def z_blocks(received, tile):
-    rows = [48 * n + 24 * tile for n in range(NARROW)]
-    inner = swap_blocks(jnp.concatenate([received[r : r + 16] for r in rows], axis=0))
-    none = jnp.zeros((8, N), F32)
-    outer = [piece for r in rows for piece in (received[r + 16 : r + 24], none)]
-    outer = swap_blocks(jnp.concatenate(outer, axis=0))
-    return inner[:96], [outer[16 * b : 16 * b + 8] for b in range(6)]
+def z_blocks(received):
+    def pick(tile, first, count):
+        return [received[48 * n + 24 * tile + first :][:count] for n in range(NARROW)]
+
+    inner = [swap_blocks(jnp.concatenate(pick(tile, 0, 16), axis=0))[:96] for tile in range(2)]
+    outer = [piece for pair in zip(pick(0, 16, 8), pick(1, 16, 8)) for piece in pair]
+    return jnp.concatenate(inner + [swap_blocks(jnp.concatenate(outer, axis=0))[:96]], axis=0)
 
 
 def taps(field, high_ref, low_ref):
@@ -222,8 +222,8 @@
     send1, recv1, send2, recv2, send3, recv3, send4, recv4,
     part, recv5, mine, recv6, whole, out,
     vext, adv, proj, proj_own, adv_hi, adv_lo, proj_hi, proj_lo,
-    hidden, hid_hi, hid_lo, scattered, gpart, gnat, face_x, face_y, corner, gext,
-    flat, own_sem, send_sem, recv_sem, vel_send, vel_recv, e1_send, e1_recv, e2_send, e2_recv,
+    hidden, hid_hi, hid_lo, scattered, gpart, hext, face_x, face_y, corner, gext,
+    flat, own_sem, send_sem, recv_sem, vel_send, vel_recv, e1_send, e1_recv,
     load_sem, token,
     ) = refs
     w = lax.axis_index("wide")
@@ -263,20 +263,29 @@
             act(lax.rem(n + i, NARROW))
 
     member = 2 * wx + core
-    column = 16 * wy + 4 * wz + zl
+    height = 4 * wz + zl
+
+    def far_first(i):
+        return jnp.where(i < 2, 2 + i, 3 - i)
 
     def each_member(act):
         for i in (4, 5, 3, 2, 6, 7, 1):
             act(lax.rem(member + i, NARROW))
 
-    def each_column(act):
+    def each_height(act):
         def body(i, carry):
-            j = i // 4
-            oz = 8 + jnp.where(j % 2 == 1, (j + 1) // 2, -(j // 2))
-            act(lax.rem(wy + 3 - i % 4, 4) * 16 + lax.rem(4 * wz + zl + oz, 16))
+            act(lax.rem(height + 8 + jnp.where(i % 2 == 1, (i + 1) // 2, -(i // 2)), 16))
             return carry
 
-        lax.fori_loop(0, WIDE - 1, body, 0)
+        lax.fori_loop(0, 15, body, 0)
+
+    def each_level(act):
+        def body(i, carry):
+            y, x = lax.rem(wy + far_first(i // 8), 4), lax.rem(wx + far_first(i // 2 % 4), 4)
+            act(8 * y + 2 * x + lax.rem(core + 1 - i % 2, 2))
+            return carry
+
+        lax.fori_loop(0, 31, body, 0)
 
     across = (WIDE, each_wide, lambda p: (p, far), None, w)
     narrow = (NARROW, each_narrow, lambda p: (w, p), n, n)
@@ -287,12 +296,19 @@
         member,
         member,
     )
-    columns = (
-        WIDE,
-        each_column,
-        lambda p: (p // 16 * 16 + p % 16 // 4 * 4 + wx, p % 4 * 2 + core),
-        column,
-        column,
+    heights = (
+        16,
+        each_height,
+        lambda p: (16 * wy + p // 4 * 4 + wx, p % 4 * 2 + core),
+        height,
+        height,
+    )
+    level = (
+        32,
+        each_level,
+        lambda p: (p // 8 * 16 + 4 * wz + p // 2 % 4, n - core + p % 2),
+        8 * wy + member,
+        8 * wy + member,
     )
 
     barrier = pltpu.get_barrier_semaphore()
@@ -433,6 +449,9 @@
     proj[...] = jnp.zeros_like(proj)
     face_y[...] = jnp.zeros_like(face_y)
     corner[...] = jnp.zeros_like(corner)
+    gext[...] = jnp.zeros_like(gext)
+    vext[:, :, 0:6] = jnp.zeros((3, 6, 6, N), F32)
+    vext[:, :, 26:32] = jnp.zeros((3, 6, 6, N), F32)
     sublane = lax.broadcasted_iota(jnp.int32, (288, N), 0) % 16
     adv[...] = jnp.where(sublane == 3, 1.0, 0.0)
 
@@ -490,18 +509,13 @@
     got4 = exchange(3, narrow, 48, send4, recv4, 42)
 
     got4()
-    inner_rows, outer_rows = [], []
-    for tile in range(2):
-        inner, outer = z_blocks(recv4[...], tile)
-        inner_rows.append(inner)
-        outer_rows.extend(outer)
-    spectra = right(jnp.concatenate(inner_rows + outer_rows, axis=0), 1)
+    spectra = right(z_blocks(recv4[...]), 1)
     fields = dot(spectra, jnp.concatenate([tz[i] for i in range(3)], axis=0), (1, 0))
     for x in range(4):
         for place, c in enumerate(ORDER):
             block = 3 * x + place
             inner = fields[16 * block : 16 * block + 16]
-            outer = fields[192 + 8 * block : 192 + 8 * block + 8]
+            outer = fields[192 + 16 * (block % 6) + 8 * (x // 2) :][:8]
             at = 4 * x + c
             proj[at : at + 1] = outer[0:1]
             proj[pl.ds(16 + at, 16, stride=16), :] = inner
@@ -518,8 +532,9 @@
         raw = stacked(rows, cols, (1, 1))
         total = jnp.zeros((16, N), F32)
         for x in range(2):
-            for piece in split(raw[16 * x : 16 * x + 16]):
-                total = total + dot(piece, gather[kind, x], (1, 0))
+            pair = jnp.concatenate(split(raw[16 * x : 16 * x + 16]), axis=0)
+            pair = dot(pair, gather[kind, x], (1, 0))
+            total = total + pair[:16] + pair[16:]
         gradients.append(total)
     lane = lanes()
     beside = jnp.logical_and(lane >= 82, lane < 123)
@@ -548,69 +563,17 @@
     for x in range(4):
         for c in range(3):
             at = 4 * x + c
-            gnat[c, x, 7:8] = gpart[at : at + 1]
-            gnat[c, x, 8:24] = gpart[pl.ds(16 + at, 16, stride=16), :]
-            gnat[c, x, 24:25] = gpart[272 + at : 273 + at]
-    own_x, own_y = pl.ds(1, 2), pl.ds(8, 16)
-    row_0, row_7, row_8, row_23, row_24 = (pl.ds(r, 1) for r in (0, 7, 8, 23, 24))
-    e1 = copies(
-        [
-            (gnat.at[:, 3, own_y, :], face_x.at[0], (ahead_w, n)),
-            (gnat.at[:, 0, own_y, :], face_x.at[1], (behind_w, n)),
-            (gnat.at[:, own_x, row_24, :], face_y.at[0, :, :, row_0, :], (w, above)),
-            (gnat.at[:, own_x, row_7, :], face_y.at[1, :, :, row_7, :], (w, below)),
-            (gnat.at[:, 3, row_24, :], corner.at[0, :, row_0, :], (ahead_w, above)),
-            (gnat.at[:, 3, row_7, :], corner.at[1, :, row_7, :], (ahead_w, below)),
-            (gnat.at[:, 0, row_24, :], corner.at[2, :, row_0, :], (behind_w, above)),
-            (gnat.at[:, 0, row_7, :], corner.at[3, :, row_7, :], (behind_w, below)),
-        ],
-        e1_send,
-        e1_recv,
-    )
-
-    got5()
-
-    def fold(ref):
-        count = ref.shape[0] // 3
-        return [
-            jnp.sum(ref[pl.ds(row, count, stride=3), :], axis=0, keepdims=True) for row in range(3)
-        ]
-
-    for row, total in enumerate(fold(recv5)):
-        mine[row : row + 1] = total
-    got6 = exchange(5, columns, 3, mine, recv6)
-
-    for copy in e1:
-        copy.wait_recv()
+            gext[c, x + 1, 7:8] = gpart[at : at + 1]
+            middle = gpart[pl.ds(16 + at, 16, stride=16), :]
+            gext[c, x + 1, 8:24] = middle + proj_own[c, x - 1] if x in (1, 2) else middle
+            gext[c, x + 1, 24:25] = gpart[272 + at : 273 + at]
+
     for c in range(3):
-        for x in range(2):
-            own = proj_own[c, x] + gnat[c, x + 1, 8:24] + face_x[x, c]
-            start = own[0:8] + face_y[0, c, x] + corner[2 * x, c]
-            end = own[8:16] + face_y[1, c, x] + corner[2 * x + 1, c]
-            gext[c, x + 1, 8:16] = start
-            gext[c, x + 1, 16:24] = end
-    e2 = copies(
-        [
-            (gext.at[:, 1, own_y, :], gext.at[:, 3, own_y, :], (behind_w, n)),
-            (gext.at[:, 2, own_y, :], gext.at[:, 0, own_y, :], (ahead_w, n)),
-            (gext.at[:, own_x, row_8, :], gext.at[:, own_x, row_24, :], (w, below)),
-            (gext.at[:, own_x, row_23, :], gext.at[:, own_x, row_7, :], (w, above)),
-        ],
-        e2_send,
-        e2_recv,
-    )
-    got6()
-    for row, total in enumerate(fold(recv6)):
-        whole[row : row + 1] = total * (N * N * N) ** -0.5
-    got7 = exchange(6, members, 3, whole, sums_hbm)
-
-    for copy in e2:
-        copy.wait_recv()
-
-    for x in range(2):
-        vx, gx = x + 2, x + 1
-        v = [vext[c, vx] for c in range(3)]
-        g = [gext[c, gx] for c in range(3)]
+        hext[c, 0] = STEP * (jnp.maximum(vext[0, 1], 0.0) * gext[c, 1])
+        hext[c, 5] = -STEP * (jnp.minimum(vext[0, 4], 0.0) * gext[c, 4])
+    for x in range(1, 5):
+        v = [vext[c, x] for c in range(3)]
+        g = [gext[c, x] for c in range(3)]
         positive = [jnp.maximum(a, 0.0) for a in v]
         negative = [jnp.minimum(a, 0.0) for a in v]
         totals = [jnp.zeros((32, N), F32)] * 3
@@ -620,9 +583,9 @@
             for c in range(3):
                 here = (positive[j] - negative[j]) * g[c]
                 if j == 0:
-                    ahead = jnp.maximum(vext[0, vx + 1], 0.0) * gext[c, gx + 1]
-                    behind = jnp.minimum(vext[0, vx - 1], 0.0) * gext[c, gx - 1]
-                    before, after = vext[c, vx - 1], vext[c, vx + 1]
+                    ahead = jnp.maximum(vext[0, x + 1], 0.0) * gext[c, x + 1]
+                    behind = jnp.minimum(vext[0, x - 1], 0.0) * gext[c, x - 1]
+                    before, after = vext[c, x - 1], vext[c, x + 1]
                 elif j == 1:
                     ahead = shift_rows(positive[1] * g[c], -1)
                     behind = shift_rows(negative[1] * g[c], 1)
@@ -633,27 +596,71 @@
                     before, after = roll(v[c], 1), roll(v[c], -1)
                 totals[c] = totals[c] + here - ahead + behind
                 rising, falling = v[c] - before, after - v[c]
-                level = 0.5 * (rising + falling)
+                level_slope = 0.5 * (rising + falling)
                 slope = slope + g[c] * jnp.where(
-                    v[j] > 0.0, rising, jnp.where(v[j] < 0.0, falling, level)
+                    v[j] > 0.0, rising, jnp.where(v[j] < 0.0, falling, level_slope)
                 )
             slopes.append(slope)
         for c in range(3):
-            out[c, x] = (g[c] - STEP * totals[c] - STEP * slopes[c])[8:24]
-
+            hext[c, x] = g[c] - STEP * totals[c] - STEP * slopes[c]
+
+    got5()
+
+    def fold(ref):
+        count = ref.shape[0] // 3
+        return [
+            jnp.sum(ref[pl.ds(row, count, stride=3), :], axis=0, keepdims=True) for row in range(3)
+        ]
+
+    for row, total in enumerate(fold(recv5)):
+        mine[row : row + 1] = total
+    got6 = exchange(5, heights, 3, mine, recv6)
+
+    before_x, own_x, after_x = pl.ds(0, 2), pl.ds(2, 2), pl.ds(4, 2)
+    before_y, own_y, after_y = pl.ds(6, 2), pl.ds(8, 16), pl.ds(24, 2)
+    first_y, last_y = pl.ds(0, 2), pl.ds(6, 2)
+    shared = copies(
+        [
+            (hext.at[:, after_x, own_y, :], face_x.at[0], (ahead_w, n)),
+            (hext.at[:, before_x, own_y, :], face_x.at[1], (behind_w, n)),
+            (hext.at[:, own_x, after_y, :], face_y.at[0, :, :, first_y, :], (w, above)),
+            (hext.at[:, own_x, before_y, :], face_y.at[1, :, :, last_y, :], (w, below)),
+            (hext.at[:, after_x, after_y, :], corner.at[0, :, :, first_y, :], (ahead_w, above)),
+            (hext.at[:, after_x, before_y, :], corner.at[1, :, :, last_y, :], (ahead_w, below)),
+            (hext.at[:, before_x, after_y, :], corner.at[2, :, :, first_y, :], (behind_w, above)),
+            (hext.at[:, before_x, before_y, :], corner.at[3, :, :, last_y, :], (behind_w, below)),
+        ],
+        e1_send,
+        e1_recv,
+    )
+
+    got6()
+    for row, total in enumerate(fold(recv6)):
+        whole[row : row + 1] = total * (N * N * N) ** -0.5
+    got7 = exchange(6, level, 3, whole, sums_hbm)
+
+    for copy in shared:
+        copy.wait_recv()
+    for c in range(3):
+        for x in range(2):
+            own = hext[c, x + 2, 8:24] + face_x[0, c, x] + face_x[1, c, x]
+            out[c, x, 0:8] = own[0:8] + face_y[0, c, x] + corner[0, c, x] + corner[2, c, x]
+            out[c, x, 8:16] = own[8:16] + face_y[1, c, x] + corner[1, c, x] + corner[3, c, x]
     store = pltpu.make_async_copy(out, out_hbm, load_sem.at[7 + TABLES])
     store.start()
+    for wait in pending[:-1]:
+        wait()
+    store.wait()
     got7()
-    store.wait()
-    for wait in pending:
-        wait()
+    pending[-1]()
 
 
 def hand_out(grad, sums, out, out_first, out_bias, out_second):
     out[...] = grad[...]
     lane = lanes()
-    spare = jnp.where(lane < 41, roll(sums[0:8], -82), roll(sums[8:16], -41))
-    both = (sums[0:16], jnp.concatenate([sums[16:24], spare], axis=0))
+    total = sums[0:24] + sums[24:48] + sums[48:72] + sums[72:96]
+    spare = jnp.where(lane < 41, roll(total[0:8], -82), roll(total[8:16], -41))
+    both = (total[0:16], jnp.concatenate([total[16:24], spare], axis=0))
     for kind, ref in enumerate((out_first, out_second)):
         turned = both[kind].T
         for tap in range(27):
@@ -677,7 +684,7 @@
     )
     results = pl.pallas_call(
         kernel,
-        out_shape=(shapes[0], jax.ShapeDtypeStruct((24, N), F32)),
+        out_shape=(shapes[0], jax.ShapeDtypeStruct((96, N), F32)),
         in_specs=[anywhere] * (7 + TABLES),
         out_specs=(anywhere,) * 2,
         scratch_shapes=[
@@ -685,15 +692,15 @@
             v(3, 3, 3, 3, 16), v(1, 16), v(3, 3, 3, 3, 16),
             *[v(*t.shape, kind=BF16) for t in constants],
             v(128, N), v(128, N), v(128, N), v(128, N), v(192, N), v(192, N), v(384, N), v(384, N),
-            v(24, N), v(24, N), v(3, N), v(192, N), v(3, N), v(3, 2, 16, N),
+            v(24, N), v(24, N), v(3, N), v(48, N), v(3, N), v(3, 2, 16, N),
             v(3, 6, 32, N), v(288, N), v(288, N), v(3, 2, 16, N),
             v(144, 2048, kind=BF16), v(144, 2048, kind=BF16),
             v(144, 2048, kind=BF16), v(144, 2048, kind=BF16),
             v(32, 2048), v(32, 2048, kind=BF16), v(32, 2048, kind=BF16),
-            v(144, 2048), v(288, N), v(3, 4, 32, N),
-            v(2, 3, 16, N), v(2, 3, 2, 8, N), v(4, 3, 8, N), v(3, 4, 32, N),
+            v(144, 2048), v(288, N), v(3, 6, 32, N),
+            v(2, 3, 2, 16, N), v(2, 3, 2, 8, N), v(4, 3, 2, 8, N), v(3, 6, 32, N),
             v(N, N), dma((7,)), dma((7,)), dma((7,)), dma((8,)), dma((8,)), dma((8,)), dma((8,)),
-            dma((4,)), dma((4,)), dma((8 + TABLES,)), pltpu.SemaphoreType.REGULAR,
+            dma((8 + TABLES,)), pltpu.SemaphoreType.REGULAR,
         ],
         compiler_params=pltpu.CompilerParams(
             collective_id=0, has_side_effects=True, vmem_limit_bytes=60 * 1024 * 1024

time: 67.7 us -> 67.2 us (level)
  no operation moved by 1% of the time
where the time goes in v4:
time: 67.2 us; the launch traced here: 67 us
  Pallas kernels  66.3 us (99%)
    pallas_call x1, Pallas kernels, local(): pl.pallas_call(kernel, out_shape=(shapes[0], jax.ShapeDtypeStruct((96, N)...  64.7 us
    pallas_call x1, Pallas kernels, local(): pl.pallas_call(hand_out, out_shape=shapes, in_specs=[in_vmem] * 2, out_sp...  1.61 us

profile of v4, /device:TPU:1, one launch (start us, length us, event | category | flops | bytes accessed | tf_op | source)
XLA Modules:
  0.0 67.0 jit_solution(2879477348584439287)
XLA Ops:
  0.6 64.7 %step_backward.1 = (f32[3,2,16,128]{3,2,1,0:T(8,128)}, f32[96,128]{1,0:T(8,128)}) custom-call(f32[4,3,2,16,128]{4,3,2,1,0:T(8,128)} %cot_hbm.1, f32[3,2,16,128]{3,2,1,0:T(8,128)} %vel_hbm.1, f32[8]{0:T(128)} %table_hbm.1, s32[4]{0:T(128)} %index_hbm.1, f32[3,3,3,3,16]{4,3,2,1,0:T(4,128)} %bitcast.6, f32[1,16]{1,0:T(1,128)} %bitcast.8, ...), custom_call_target="tpu_custom_call" | custom-call | tf_op jit(solution)/shard_map/step_backward/pallas_call | solution.py:685
  65.3 1.6 %hand_out.1 = (f32[3,2,16,128]{3,2,1,0:T(8,128)}, f32[3,3,3,3,16]{4,3,2,1,0:T(4,128)}, f32[1,16]{1,0:T(1,128)}, f32[3,3,3,3,16]{4,3,2,1,0:T(4,128)}) custom-call(f32[3,2,16,128]{3,2,1,0:T(8,128)} %get-tuple-element.10.grad, f32[96,128]{1,0:T(8,128)} %get-tuple-element.11.sums), custom_call_target="tpu_custom_call" | custom-call | tf_op jit(solution)/shard_map/hand_out/pallas_call | solution.py:714

commit v5 on v4

--- a/solution.py
+++ b/solution.py
@@ -237,26 +237,23 @@
     longer = jnp.where(zl < 2, 1, 3)
 
     def each_wide(act):
-        def offset(i):
-            return jnp.where(i < 2, 2 + i, 3 - i)
-
+        ys = [lax.rem(wy + i, 4) * 16 for i in (2, 3, 1, 0)]
+        xs = [lax.rem(wx + i, 4) for i in (2, 3, 1, 0)]
         for pair in ((2, longer), (0, lax.rem(longer + 2, 4))):
             zs = [lax.rem(wz + oz, 4) * 4 for oz in pair]
 
-            def body(i, carry, zs=zs):
-                place = lax.rem(wy + offset(i // 4), 4) * 16 + lax.rem(wx + offset(i % 4), 4)
-                for z in zs:
-                    act(place + z)
-                return carry
-
-            lax.fori_loop(0, 16, body, 0)
+            for y in ys:
+                for x in xs:
+                    for z in zs:
+                        act(y + x + z)
 
     def each_plane(act):
         def body(i, carry):
-            act(lax.rem(wy + i // 4, 4) * 16 + wz * 4 + lax.rem(wx + i % 4, 4))
+            y, x = lax.rem(wy + far_first(i // 4), 4), lax.rem(wx + far_first(i % 4), 4)
+            act(y * 16 + wz * 4 + x)
             return carry
 
-        lax.fori_loop(1, 16, body, 0)
+        lax.fori_loop(0, 15, body, 0)
 
     def each_narrow(act):
         for i in (4, 5, 3, 2, 6, 7, 1):

time: 67.2 us -> 66.9 us (level)
  no operation moved by 1% of the time
where the time goes in v5:
time: 66.9 us; the launch traced here: 66.7 us
  Pallas kernels  66.1 us (99%)
    pallas_call x1, Pallas kernels, local(): pl.pallas_call(kernel, out_shape=(shapes[0], jax.ShapeDtypeStruct((96, N)...  64.4 us
    pallas_call x1, Pallas kernels, local(): pl.pallas_call(hand_out, out_shape=shapes, in_specs=[in_vmem] * 2, out_sp...  1.61 us

profile of v5, /device:TPU:1, one launch (start us, length us, event | category | flops | bytes accessed | tf_op | source)
XLA Modules:
  0.0 66.7 jit_solution(16786323500670823124)
XLA Ops:
  0.6 64.4 %step_backward.1 = (f32[3,2,16,128]{3,2,1,0:T(8,128)}, f32[96,128]{1,0:T(8,128)}) custom-call(f32[4,3,2,16,128]{4,3,2,1,0:T(8,128)} %cot_hbm.1, f32[3,2,16,128]{3,2,1,0:T(8,128)} %vel_hbm.1, f32[8]{0:T(128)} %table_hbm.1, s32[4]{0:T(128)} %index_hbm.1, f32[3,3,3,3,16]{4,3,2,1,0:T(4,128)} %bitcast.6, f32[1,16]{1,0:T(1,128)} %bitcast.8, ...), custom_call_target="tpu_custom_call" | custom-call | tf_op jit(solution)/shard_map/step_backward/pallas_call | solution.py:682
  65.1 1.6 %hand_out.1 = (f32[3,2,16,128]{3,2,1,0:T(8,128)}, f32[3,3,3,3,16]{4,3,2,1,0:T(4,128)}, f32[1,16]{1,0:T(1,128)}, f32[3,3,3,3,16]{4,3,2,1,0:T(4,128)}) custom-call(f32[3,2,16,128]{3,2,1,0:T(8,128)} %get-tuple-element.10.grad, f32[96,128]{1,0:T(8,128)} %get-tuple-element.11.sums), custom_call_target="tpu_custom_call" | custom-call | tf_op jit(solution)/shard_map/hand_out/pallas_call | solution.py:711
